TPU v7x, 32 devices: a whole 2x2x4 slice. The times are simulated.
32 devices in a mesh: section: 2 (over y), row: 4 (over x, core), col: 4 (over z).
Axes of the slice: x: 2, y: 2, z: 4, core: 2. Of those that a mesh axis runs over, the one named last changes fastest.
Arguments:
- hidden_in: bfloat16 [2, 128, 8192], P('section', 'col', 'row'), may hold values from -600 to 600
- norm_gain: float32 [2, 8192], P('section', 'row'), may hold values from 0.1 to 1.9
- q_weight: bfloat16 [2, 8192, 8192], P('section', 'row', 'col'), may hold values from -0.0625 to 0.0625
- kv_weight: bfloat16 [2, 8192, 2048], P('section', 'row', 'col'), may hold values from -0.0625 to 0.0625
- kv_cache: bfloat16 [2, 8, 1024, 2, 1024], P('section', 'col', 'row'), may hold values from -110 to 110
- lengths: int32 [2, 8], P('section', 'col'), may hold values from 768 to 1024, as said below
Outputs:
- handed: bfloat16 [2, 128, 8192], P('section', 'col', 'row')
- new_kv: bfloat16 [2, 128, 2048], P('section', 'col')
Inputs may be any that keep to these rules, and one draw needn't show every extreme that they name: `lengths`: in every section some prompt uses exactly 1024 positions.
All inputs are finite; a program needn't handle non-finite values.
Results may differ from a plain program's by a relative error of at most 0.023.
Values may be sent and summed in bfloat16 or wider, within the bound.
A program may use at most 64 MiB of HBM per device.

v0:
```python
import jax
import jax.numpy as jnp
from jax import lax
from jax.sharding import PartitionSpec as P

HEAD_DIM = 128


EPSILON = 1e-05
FLOOR = -1e30


def combined_all(value, axis, combine):
    everything = jax.tree.map(
        lambda part, kind: lax.all_gather(part.astype(kind), axis),
        value,
        (jnp.bfloat16, jnp.bfloat16, jnp.bfloat16),
    )

    def take(k):
        return jax.tree.map(lambda part, own: part[k].astype(own.dtype), everything, value)

    return lax.fori_loop(
        1, lax.axis_size(axis), lambda k, so_far: combine(so_far, take(k)), take(0)
    )


def shifted(block, axis, distance):
    devices = range(lax.axis_size(axis))
    route = [((i - distance) % len(devices), i) for i in devices]
    return lax.ppermute(block, axis, route)


def join_parts(former, latter):
    top_score = jnp.maximum(former[0], latter[0])
    keep_former = jnp.exp(former[0] - top_score)
    keep_latter = jnp.exp(latter[0] - top_score)
    return (
        top_score,
        former[1] * keep_former + latter[1] * keep_latter,
        former[2] * keep_former[..., None] + latter[2] * keep_latter[..., None],
    )


def finish(run_max, run_total, run_out, own_score, own_values):
    top_score = jnp.maximum(run_max, own_score)
    keep_part = jnp.exp(run_max - top_score)
    own_weight = jnp.exp(own_score - top_score)
    total_weight = run_total * keep_part + own_weight
    own_rounded = lax.optimization_barrier(own_weight.astype(jnp.bfloat16)).astype(jnp.float32)
    numerator = run_out * keep_part[..., None] + own_rounded[..., None] * own_values.astype(
        jnp.float32
    )
    attended = (numerator / total_weight[..., None]).astype(jnp.bfloat16)
    return attended.reshape(attended.shape[0], -1)


def shards(hidden_in, norm_gain, q_weight, kv_weight, kv_cache, lengths):
    row_count = lax.axis_size("row")
    col_count = lax.axis_size("col")
    row_index = lax.axis_index("row")
    rows_here = hidden_in.shape[1]
    width_part = hidden_in.shape[2]
    sub_rows = rows_here // row_count
    widened = hidden_in[0].astype(jnp.float32)
    squares = lax.psum(jnp.sum(widened * widened, axis=1), "row")
    scaling = lax.rsqrt(squares / (width_part * row_count) + EPSILON)
    normed = (widened * scaling[:, None] * norm_gain[0][None, :]).astype(jnp.bfloat16)
    gathered = lax.all_gather(
        normed.reshape(row_count, sub_rows, width_part), "col", axis=1, tiled=True
    )
    query_weight = q_weight[0]
    pair_weight = kv_weight[0]
    query_cols = query_weight.shape[1]
    pair_cols = pair_weight.shape[1]
    lead_shape = gathered.shape[:-1]
    flat_rows = gathered.reshape(-1, width_part)
    query_part = jnp.dot(flat_rows, query_weight, preferred_element_type=jnp.float32).reshape(
        lead_shape + (query_cols,)
    )
    pair_part = jnp.dot(flat_rows, pair_weight, preferred_element_type=jnp.float32).reshape(
        lead_shape + (pair_cols,)
    )
    query_part, pair_part = (query_part, pair_part)
    query_total, pair_total = lax.psum((query_part, pair_part), "row")
    query_blocks = query_total.astype(jnp.bfloat16).reshape(
        row_count, col_count, sub_rows, query_cols
    )
    pair_blocks = pair_total.astype(jnp.bfloat16).reshape(row_count, col_count, sub_rows, pair_cols)
    query_mine, pair_mine = (
        lax.all_to_all(query_blocks, "col", split_axis=1, concat_axis=3, tiled=True),
        lax.all_to_all(pair_blocks, "col", split_axis=1, concat_axis=3, tiled=True),
    )
    query = query_mine.reshape(rows_here, -1)
    new_kv = pair_mine.reshape(rows_here, -1)
    prompts_here = lengths.shape[1]
    samples = rows_here // prompts_here
    key_heads = new_kv.shape[1] // (2 * HEAD_DIM)
    head_count = query.shape[1] // HEAD_DIM
    group_size = head_count // key_heads
    score_scale = HEAD_DIM ** (-0.5)
    query_heads = query.reshape(prompts_here, samples, key_heads, group_size, HEAD_DIM)
    cache_local = kv_cache[0]
    positions_here = cache_local.shape[1]
    cache_keys = cache_local[:, :, 0].reshape(prompts_here, positions_here, key_heads, HEAD_DIM)
    cache_values = cache_local[:, :, 1].reshape(prompts_here, positions_here, key_heads, HEAD_DIM)
    scores = (
        jnp.einsum("psghd,ptgd->psght", query_heads, cache_keys, preferred_element_type=jnp.float32)
        * score_scale
    )
    positions = row_index * positions_here + jnp.arange(positions_here, dtype=jnp.int32)
    in_range = (positions[None, :] < lengths[0][:, None])[:, None, None, None, :]
    local_max = jnp.max(jnp.where(in_range, scores, FLOOR), axis=-1)
    weights = jnp.where(in_range, jnp.exp(scores - local_max[..., None]), 0.0)
    local_total = jnp.sum(weights, axis=-1)
    local_out = jnp.einsum(
        "psght,ptgd->psghd",
        weights.astype(jnp.bfloat16),
        cache_values,
        preferred_element_type=jnp.float32,
    )
    new_keys = new_kv[:, : key_heads * HEAD_DIM].reshape(prompts_here, samples, key_heads, HEAD_DIM)
    new_values = new_kv[:, key_heads * HEAD_DIM :].reshape(rows_here, key_heads, 1, HEAD_DIM)
    own_score = (
        jnp.einsum("psghd,psgd->psgh", query_heads, new_keys, preferred_element_type=jnp.float32)
        * score_scale
    )
    own_score = own_score.reshape(rows_here, head_count)
    own_values = jnp.broadcast_to(new_values, (rows_here, key_heads, group_size, HEAD_DIM)).reshape(
        rows_here, head_count, HEAD_DIM
    )
    part_heads = head_count // row_count
    first_head = row_index * part_heads
    flat_max = local_max.reshape(rows_here, head_count)
    flat_total = local_total.reshape(rows_here, head_count)
    flat_out = local_out.reshape(rows_here, head_count, HEAD_DIM)
    joined = combined_all((flat_max, flat_total, flat_out), "row", join_parts)
    run_max = lax.dynamic_slice_in_dim(joined[0], first_head, part_heads, 1)
    run_total = lax.dynamic_slice_in_dim(joined[1], first_head, part_heads, 1)
    run_out = lax.dynamic_slice_in_dim(joined[2], first_head, part_heads, 1)
    mine_score = lax.dynamic_slice_in_dim(own_score, first_head, part_heads, 1)
    mine_values = lax.dynamic_slice_in_dim(own_values, first_head, part_heads, 1)
    attended = finish(run_max, run_total, run_out, mine_score, mine_values)
    handed = shifted(attended[None], "section", 1)
    return (handed, new_kv[None])


def solution(mesh):
    return jax.shard_map(
        shards,
        mesh=mesh,
        in_specs=(
            P("section", "col", "row"),
            P("section", "row"),
            P("section", "row", "col"),
            P("section", "row", "col"),
            P("section", "col", "row", None, None),
            P("section", "col"),
        ),
        out_specs=(P("section", "col", "row"), P("section", "col", None)),
        check_vma=False,
    )
```

profile of v0, /device:TPU:2, one launch (start us, length us, event | category | flops | bytes accessed | tf_op | source)
XLA Modules:
  0.0 142.7 jit_solution(7552088394451358546)
XLA Ops:
  7.2 1.2 fusion.24
  8.4 5.8 %psum.21 = f32[32]{0:T(128)S(1)} all-reduce(f32[32]{0:T(128)S(1)} %fusion.24), channel_id=1, replica_groups=mesh['section'=2,'row'=4,'col'=4] {'row'}, use_global_device_ids=true, to_apply=%region_1.0 | all-reduce | flops 32 | bytes 256 | tf_op jit(solution)/shard_map/psum | solution.py:66
  14.1 0.1 mul.140
  14.2 1.0 fusion.23
  15.2 16.0 %all_gather.15 = bf16[4,32,2048]{2,1,0:T(8,128)(2,1)S(1)} all-gather(bf16[4,8,2048]{2,1,0:T(8,128)(2,1)S(1)} %fusion.23), channel_id=1, replica_groups=mesh['section'=2,'row'=4,'col'=4] {'col'}, dimensions={1}, use_global_device_ids=true | all-gather | bytes 655360 | tf_op jit(solution)/shard_map/all_gather | solution.py:69
  31.3 4.7 %fusion.3 = f32[4,32,2048]{2,1,0:T(8,128)S(1)} fusion(bf16[4,32,2048]{2,1,0:T(8,128)(2,1)S(1)} %all_gather.15, bf16[1,2048,2048]{2,1,0:T(8,128)(2,1)} %param.10), kind=kOutput, calls=%fused_computation.8 | convolution fusion | flops 1073741824 | bytes 9961472 | tf_op jit(solution)/shard_map/dot_general | solution.py:78
  35.9 0.5 fusion.5
  36.4 27.1 %all-reduce.2 = (bf16[4,32,2048]{2,1,0:T(8,128)(2,1)}, bf16[4,32,512]{2,1,0:T(8,128)(2,1)S(1)}) all-reduce(f32[4,32,2048]{2,1,0:T(8,128)S(1)} %fusion.3, f32[4,32,512]{2,1,0:T(8,128)S(1)} %fusion.5), channel_id=1, replica_groups=mesh['section'=2,'row'=4,'col'=4] {'row'}, use_global_device_ids=true, to_apply=%region_2.0 | all-reduce | flops 327680 | bytes 1966080 | tf_op jit(solution)/shard_map/psum | solution.py:85
  63.5 1.9 %copy.61 = bf16[4,4,8,2048]{3,2,0,1:T(8,128)(2,1)} copy(bf16[4,4,8,2048]{3,2,1,0:T(8,128)(2,1)} %bitcast.122) | data formatting | bytes 1048576 | tf_op jit(solution)/shard_map/reshape | solution.py:86
  65.4 6.3 %all-to-all-start = ((bf16[4,4,8,2048]{3,2,0,1:T(8,128)(2,1)}), bf16[4,4,8,2048]{3,2,0,1:T(8,128)(2,1)}, u32[]{:S(2)}, u32[]{:S(2)}) async-start(bf16[4,4,8,2048]{3,2,0,1:T(8,128)(2,1)} %copy.61), calls=%async_computation | async-start | bytes 1048576 | tf_op jit(solution)/shard_map/all_to_all | solution.py:91
  71.7 6.1 %copy.63 = bf16[1,2,256,2,1024]{2,4,1,3,0:T(8,128)(2,1)} copy(bf16[1,2,256,2,1024]{4,3,2,1,0:T(2,128)(2,1)} %param.12) | data formatting | bytes 4194304 | tf_op args[4]
  77.8 2.7 %fusion.34 = (bf16[2,256,1,1024]{1,3,0,2:T(8,128)(2,1)}, bf16[2,256,1,1024]{1,3,0,2:T(8,128)(2,1)S(1)}) fusion(bf16[2,256,2,1024]{1,3,0,2:T(8,128)(2,1)} %bitcast.117), kind=kLoop, calls=%fused_computation.57 | loop fusion | bytes 4194304 | tf_op jit(solution)/shard_map/slice | solution.py:106
  80.5 6.2 %all-to-all-done = bf16[4,4,8,2048]{3,2,0,1:T(8,128)(2,1)} async-done(((bf16[4,4,8,2048]{3,2,0,1:T(8,128)(2,1)}), bf16[4,4,8,2048]{3,2,0,1:T(8,128)(2,1)}, u32[]{:S(2)}, u32[]{:S(2)}) %all-to-all-start) | async-done | bytes 524320 | tf_op jit(solution)/shard_map/all_to_all | solution.py:91
  86.7 2.3 %copy.62 = bf16[4,1,8,4,2048]{4,3,2,0,1:T(4,128)(2,1)} copy(bf16[4,1,8,4,2048]{4,2,0,3,1:T(8,128)(2,1)} %bitcast.11) | data formatting | bytes 1048576 | tf_op jit(solution)/shard_map/all_to_all | solution.py:91
  89.0 2.2 %reshape_reshape.3 = bf16[2,16,8,8,128]{4,3,2,1,0:T(8,128)(2,1)} reshape(bf16[4,1,8,4,2048]{4,3,2,0,1:T(4,128)(2,1)} %copy.62) | data formatting | bytes 1048576 | tf_op jit(solution)/shard_map/reshape;reshape | solution.py:102
  91.2 1.7 %fusion.7 = (f32[2,16,8,8]{3,1,2,0:T(8,128)S(1)}, f32[2,8,16,8,256]{4,3,2,1,0:T(8,128)S(1)}) fusion(pred[2,256]{1,0:T(4,128)(4,1)S(1)} %broadcast_compare_fusion, bf16[2,256,8,128,1]{1,3,4,2,0:T(8,128)(2,1)S(1)} %bitcast.118, bf16[2,16,8,8,128]{4,3,2,1,0:T(8,128)(2,1)} %reshape_reshape.3), kind=kOutput, calls=%fused_computation.14 | convolution fusion | flops 135788544 | bytes 3678720 | tf_op jit(solution)/shard_map/psghd,ptgd->psght/dot_general | solution.py:108
  92.9 0.6 fusion.12
  93.5 0.7 copy-done.1
  94.1 1.0 copy.73
  95.1 0.7 copy.75
  95.8 3.3 %all-to-all-start.1 = ((bf16[4,4,8,512]{3,2,0,1:T(8,128)(2,1)}), bf16[4,4,8,512]{3,2,0,1:T(8,128)(2,1)S(1)}, u32[]{:S(2)}, u32[]{:S(2)}) async-start(bf16[4,4,8,512]{3,2,0,1:T(8,128)(2,1)} %copy.75), calls=%async_computation.1 | async-start | bytes 262144 | tf_op jit(solution)/shard_map/all_to_all | solution.py:92
  99.1 5.9 %all-to-all-done.1 = bf16[4,4,8,512]{3,2,0,1:T(8,128)(2,1)S(1)} async-done(((bf16[4,4,8,512]{3,2,0,1:T(8,128)(2,1)}), bf16[4,4,8,512]{3,2,0,1:T(8,128)(2,1)S(1)}, u32[]{:S(2)}, u32[]{:S(2)}) %all-to-all-start.1) | async-done | bytes 131104 | tf_op jit(solution)/shard_map/all_to_all | solution.py:92
  105.0 0.1 copy.98
  105.3 0.9 broadcast_bitcast_fusion
  106.2 0.1 copy.66
  106.3 0.1 convert_element_type.140
  106.4 0.1 copy.68
  106.5 2.3 %fusion.11 = bf16[2,16,8,8]{3,1,2,0:T(8,128)(2,1)S(1)} fusion(f32[2,8,16,8,256]{4,3,2,1,0:T(8,128)} %copy-done.1, f32[2,16,8,8]{3,1,2,0:T(8,128)S(1)} %get-tuple-element.219, pred[2,256]{1,0:T(4,128)(4,1)S(1)} %broadcast_compare_fusion), kind=kLoop, calls=%fused_computation.18 | loop fusion | flops 2095104 | bytes 2109952 | tf_op jit(solution)/shard_map/reduce_sum | solution.py:115
  108.8 0.1 copy.69
  109.0 0.1 convert_element_type.144
  109.0 0.1 copy.71
  109.1 0.4 fusion.36
  109.6 0.1 copy.85
  109.7 0.1 reshape.139
  109.8 5.3 %all_gather.16 = bf16[4,32,64]{2,1,0:T(8,128)(2,1)S(1)} all-gather(bf16[1,32,64]{2,1,0:T(8,128)(2,1)S(1)} %copy.68), channel_id=1, replica_groups=mesh['section'=2,'row'=4,'col'=4] {'row'}, dimensions={0}, use_global_device_ids=true | all-gather | bytes 20480 | tf_op jit(solution)/shard_map/all_gather | solution.py:15
  115.2 5.2 %all_gather.17 = bf16[4,32,64]{2,1,0:T(8,128)(2,1)S(1)} all-gather(bf16[1,32,64]{2,1,0:T(8,128)(2,1)S(1)} %copy.71), channel_id=1, replica_groups=mesh['section'=2,'row'=4,'col'=4] {'row'}, dimensions={0}, use_global_device_ids=true | all-gather | bytes 20480 | tf_op jit(solution)/shard_map/all_gather | solution.py:15
  120.4 1.1 fusion.18
  121.5 6.2 %while.19 = (s32[]{:T(128)}, f32[32,64]{1,0:T(8,128)S(1)}, f32[32,64]{1,0:T(8,128)S(1)}, f32[32,64,128]{2,1,0:T(8,128)S(1)}, bf16[4,32,64]{2,1,0:T(8,128)(2,1)S(...) while((s32[]{:T(128)}, f32[32,64]{1,0:T(8,128)S(1)}, ...), condition=%wide.region_6.7_spmd, body=%wide.region_5.6_spmd.sunk | while | flops 1064965 | bytes 2695319 | solution.py:23
  121.6 2.0 %fusion.46 = f32[32,64,128]{2,1,0:T(8,128)S(1)} fusion(f32[32,64,128]{2,1,0:T(8,128)S(1)} %get-tuple-element.285, f32[32,64]{1,0:T(8,128)S(1)} %get-tuple-element.270, bf16[4,32,64,128]{3,2,1,0:T(8,128)(2,1)} %get-tuple-element.298, s32[]{:T(128)S(6)} %select_n.39, f32[32,64]{1,0:T(8,128)S(1)} %get-tuple-element.271), kind=kLoop, calls=%fused_computation.1.clone.1 | loop fusion | flops 1048576 | bytes 2637828 | tf_op jit(solution)/shard_map/while/body/eval_jaxpr/add | solution.py:41
  123.6 2.0 %fusion.46 = f32[32,64,128]{2,1,0:T(8,128)S(1)} fusion(f32[32,64,128]{2,1,0:T(8,128)S(1)} %get-tuple-element.285, f32[32,64]{1,0:T(8,128)S(1)} %get-tuple-element.270, bf16[4,32,64,128]{3,2,1,0:T(8,128)(2,1)} %get-tuple-element.298, s32[]{:T(128)S(6)} %select_n.39, f32[32,64]{1,0:T(8,128)S(1)} %get-tuple-element.271), kind=kLoop, calls=%fused_computation.1.clone.1 | loop fusion | flops 1048576 | bytes 2637828 | tf_op jit(solution)/shard_map/while/body/eval_jaxpr/add | solution.py:41
  125.7 2.0 %fusion.46 = f32[32,64,128]{2,1,0:T(8,128)S(1)} fusion(f32[32,64,128]{2,1,0:T(8,128)S(1)} %get-tuple-element.285, f32[32,64]{1,0:T(8,128)S(1)} %get-tuple-element.270, bf16[4,32,64,128]{3,2,1,0:T(8,128)(2,1)} %get-tuple-element.298, s32[]{:T(128)S(6)} %select_n.39, f32[32,64]{1,0:T(8,128)S(1)} %get-tuple-element.271), kind=kLoop, calls=%fused_computation.1.clone.1 | loop fusion | flops 1048576 | bytes 2637828 | tf_op jit(solution)/shard_map/while/body/eval_jaxpr/add | solution.py:41
  127.7 0.1 copy.79
  127.9 0.1 copy.78
  128.1 1.2 divide_convert_fusion
  129.4 1.6 %collective-permute-start = (bf16[1,32,2048]{2,1,0:T(8,128)(2,1)S(1)}, bf16[1,32,2048]{2,1,0:T(8,128)(2,1)S(1)}, u32[]{:S(2)}, u32[]{:S(2)}) collective-permute-start(bf16[1,32,2048]{2,1,0:T(8,128)(2,1)S(1)} %broadcast_in_dim_reshape.6), channel_id=1, source_target_pairs={{16,0},{0,16},{17,1},{1,17},{18,2},{2,18},{19,3},{3,19},{20,4},{4,... | collective-permute-start | bytes 393224 | tf_op jit(solution)/shard_map/ppermute | solution.py:31
  131.0 0.7 broadcast_in_dim_reshape.7
  131.7 3.4 %collective-permute-done = bf16[1,32,2048]{2,1,0:T(8,128)(2,1)S(1)} collective-permute-done((bf16[1,32,2048]{2,1,0:T(8,128)(2,1)S(1)}, bf16[1,32,2048]{2,1,0:T(8,128)(2,1)S(1)}, u32[]{:S(2)}, u32[]{:S(2)}) %collective-permute-start) | collective-permute-done | bytes 131104 | tf_op jit(solution)/shard_map/ppermute | solution.py:31
  135.2 0.7 copy.116
  (32 shorter events, 0.7 us)
Async XLA Ops:
  7.2 28.8 %copy-start = (bf16[1,2048,512]{2,1,0:T(8,128)(2,1)S(1)}, bf16[1,2048,512]{2,1,0:T(8,128)(2,1)}, u32[]{:S(2)}) copy-start(bf16[1,2048,512]{2,1,0:T(8,128)(2,1)} %param.11) | copy-start | bytes 6291460
  65.4 21.3 %all-to-all-start = ((bf16[4,4,8,2048]{3,2,0,1:T(8,128)(2,1)}), bf16[4,4,8,2048]{3,2,0,1:T(8,128)(2,1)}, u32[]{:S(2)}, u32[]{:S(2)}) async-start(bf16[4,4,8,2048]{3,2,0,1:T(8,128)(2,1)} %copy.61), calls=%async_computation | async-start | bytes 1048576 | tf_op jit(solution)/shard_map/all_to_all | solution.py:91
  71.7 48.7 %all-gather.2.cloned.1.call-start = ((), (), s32[]{:S(2)}) async-start(), calls=%async_computation.2 | async-start | bytes 2621440 | tf_op jit(solution)/shard_map/all_gather | solution.py:15
  71.7 6.1 %copy-start.4 = (s32[1,2]{1,0:T(1,128)S(1)}, s32[1,2]{1,0:T(1,128)}, u32[]{:S(2)}) copy-start(s32[1,2]{1,0:T(1,128)} %param.13) | copy-start | bytes 28
  91.2 1.7 %copy-start.3 = (bf16[2,256,1,1024]{1,3,0,2:T(8,128)(2,1)S(1)}, bf16[2,256,1,1024]{1,3,0,2:T(8,128)(2,1)}, u32[]{:S(2)}) copy-start(bf16[2,256,1,1024]{1,3,0,2:T(8,128)(2,1)} %get-tuple-element.212) | copy-start | bytes 3145732
  92.8 1.3 copy-start.1
  95.8 9.2 %all-to-all-start.1 = ((bf16[4,4,8,512]{3,2,0,1:T(8,128)(2,1)}), bf16[4,4,8,512]{3,2,0,1:T(8,128)(2,1)S(1)}, u32[]{:S(2)}, u32[]{:S(2)}) async-start(bf16[4,4,8,512]{3,2,0,1:T(8,128)(2,1)} %copy.75), calls=%async_computation.1 | async-start | bytes 262144 | tf_op jit(solution)/shard_map/all_to_all | solution.py:92
  105.1 4.0 %copy-start.2 = (bf16[2,16,8,8,128]{4,3,2,1,0:T(8,128)(2,1)S(1)}, bf16[2,16,8,8,128]{4,3,2,1,0:T(8,128)(2,1)}, u32[]{:S(2)}) copy-start(bf16[2,16,8,8,128]{4,3,2,1,0:T(8,128)(2,1)} %reshape_reshape.3) | copy-start | bytes 1572868
  129.4 5.8 %collective-permute-start = (bf16[1,32,2048]{2,1,0:T(8,128)(2,1)S(1)}, bf16[1,32,2048]{2,1,0:T(8,128)(2,1)S(1)}, u32[]{:S(2)}, u32[]{:S(2)}) collective-permute-start(bf16[1,32,2048]{2,1,0:T(8,128)(2,1)S(1)} %broadcast_in_dim_reshape.6), channel_id=1, source_target_pairs={{16,0},{0,16},{17,1},{1,17},{18,2},{2,18},{19,3},{3,19},{20,4},{4,... | collective-permute-start | bytes 393224 | tf_op jit(solution)/shard_map/ppermute | solution.py:31
Sparse Core Ops, SparseCore 0:
  95.2 20.7 all-gather.1
where the time goes:
time: 145 us; the launch traced here: 143 us
  blocking collectives  59.4 us (41%)
  local copies, waits for them, and re-layouts  21.3 us (15%)
  waiting for transfers between devices  15.6 us (11%)
  between operations  14.2 us (10%)
  other arithmetic  13.1 us (9%)
  starting transfers between devices  11.2 us (8%)
  matrix products  7.82 us (5%)
    psum x1, blocking collectives, shards(): query_total, pair_total = lax.psum((query_part, pair_part), 'row')  27.1 us
    all_gather x1, blocking collectives, shards(): lax.all_gather(normed.reshape(row_count, sub_rows, width_part), 'col', ax...  16 us
    all_gather x2, blocking collectives, combined_all(): lax.all_gather(part.astype(kind), axis)  10.5 us
    unnamed x15, local copies, waits for them, and re-layouts  7.49 us
    all_to_all x1, starting transfers between devices, shards(): lax.all_to_all(query_blocks, 'col', split_axis=1, concat_axis=3, tiled=True)  6.27 us
    all_to_all x1, waiting for transfers between devices, shards(): lax.all_to_all(query_blocks, 'col', split_axis=1, concat_axis=3, tiled=True)  6.24 us
    add x3, other arithmetic, join_parts(): former[2] * keep_former[..., None] + latter[2] * keep_latter[..., None]  6 us
    all_to_all x1, waiting for transfers between devices, shards(): lax.all_to_all(pair_blocks, 'col', split_axis=1, concat_axis=3, tiled=True)  5.88 us
  transfers between devices with their start and end apart: 4, of which 3 were waited for; matrix products, arithmetic and copies ran while one was open for 10% of the time, Pallas kernels for 0%

commit v1 on v0

v1 whole, which is shorter than its diff:
```python
import functools

import jax
import jax.numpy as jnp
from jax import lax
from jax.experimental import pallas as pl
from jax.experimental.pallas import tpu as pltpu
from jax.sharding import PartitionSpec as P

HEAD_DIM = 128
EPSILON = 1e-05
FLOOR = -1e30
TILE = 512
MESH = pl.DeviceIdType.MESH
F32 = jnp.float32
BF16 = jnp.bfloat16


def kernel(
    dims,
    hidden_ref,
    gain_ref,
    qw_ref,
    kvw_ref,
    cache_ref,
    len_ref,
    handed_ref,
    newkv_ref,
    weights,
    cache,
    gathered,
    parts,
    arrived,
    summed,
    full,
    outs,
    outs_in,
    stat_tile,
    stat_rows,
    stat_in,
    squares,
    final,
    weight_sem,
    cache_sem,
    gather_send,
    gather_recv,
    own_send,
    sum_send,
    sum_recv,
    turn_send,
    turn_recv,
    full_send,
    full_recv,
    out_send,
    out_recv,
    stat_send,
    stat_recv,
    square_send,
    square_recv,
    hand_send,
    hand_recv,
):
    n_sec, n_row, n_col, units, quarter, heads_per, pairs_per, kv_heads = dims
    sec, row, col = lax.axis_index("section"), lax.axis_index("row"), lax.axis_index("col")
    rows, width = hidden_ref.shape
    prompts, slots = cache_ref.shape[0], cache_ref.shape[1]
    samples = rows // prompts
    group = (heads_per * n_col) // kv_heads
    tall = group * samples
    mine = kv_heads // n_row
    q_tiles = qw_ref.shape[1] // TILE
    tiles = units * HEAD_DIM // TILE
    pair_cols = kvw_ref.shape[1]

    def peer(d):
        return lax.rem(row + d, n_row)

    loads = []
    for t in range(q_tiles):
        loads.append(
            pltpu.make_async_copy(
                qw_ref.at[:, pl.ds(t * TILE, TILE)], weights.at[t], weight_sem.at[t]
            )
        )
    for t in range(q_tiles, tiles):
        first = (t - q_tiles) * TILE
        wide = min(TILE, pair_cols - first)
        if wide > 0:
            loads.append(
                pltpu.make_async_copy(
                    kvw_ref.at[:, pl.ds(first, wide)],
                    weights.at[t, :, pl.ds(0, wide)],
                    weight_sem.at[t],
                )
            )
        else:
            loads.append(None)
    for load in loads:
        if load is not None:
            load.start()
    cache_load = pltpu.make_async_copy(cache_ref, cache, cache_sem)
    cache_load.start()

    barrier = pltpu.get_barrier_semaphore()
    for d in range(1, n_row):
        pl.semaphore_signal(barrier, inc=1, device_id=(sec, peer(d), col), device_id_type=MESH)
    for d in range(1, n_col):
        pl.semaphore_signal(
            barrier, inc=1, device_id=(sec, row, lax.rem(col + d, n_col)), device_id_type=MESH
        )
    pl.semaphore_signal(
        barrier, inc=1, device_id=(lax.rem(sec + n_sec - 1, n_sec), row, col), device_id_type=MESH
    )

    for t in range(q_tiles, tiles):
        first = (t - q_tiles) * TILE
        wide = max(0, min(TILE, pair_cols - first))
        if wide < TILE:
            weights[t, :, wide:] = jnp.zeros((width, TILE - wide), BF16)
    widened = hidden_ref[...].astype(F32)
    gathered[col] = (widened * gain_ref[...]).astype(BF16)
    squares[row] = jnp.broadcast_to(
        jnp.sum(widened * widened, axis=1, keepdims=True), (rows, HEAD_DIM)
    )

    pl.semaphore_wait(barrier, n_row - 1 + n_col - 1 + 1)

    def gather_copy(block, to, send_sem):
        return pltpu.make_async_remote_copy(
            src_ref=gathered.at[block],
            dst_ref=gathered.at[block],
            send_sem=send_sem,
            recv_sem=gather_recv.at[block],
            device_id=(sec, row, to),
            device_id_type=MESH,
        )

    below, above = jnp.maximum(col - 1, 0), jnp.minimum(col + 1, n_col - 1)

    @pl.when(col > 0)
    def _():
        gather_copy(col, below, gather_send.at[col]).start()

    @pl.when(col < n_col - 1)
    def _():
        gather_copy(col, above, own_send).start()

    def square_copy(d):
        return pltpu.make_async_remote_copy(
            src_ref=squares.at[row],
            dst_ref=squares.at[row],
            send_sem=square_send.at[d],
            recv_sem=square_recv.at[row],
            device_id=(sec, peer(d), col),
            device_id_type=MESH,
        )

    for d in range(1, n_row):
        square_copy(d).start()

    shorter = jnp.minimum(col, n_col - 1 - col)
    upward = col < n_col - 1 - col

    def block_at(k):
        half = (k + 1) // 2
        near = jnp.where(k % 2 == 1, col + half, col - half)
        far = jnp.where(upward, col + (k - shorter), col - (k - shorter))
        return jnp.where(k <= 2 * shorter, near, far)

    def sum_copy(block, d):
        other = peer(d)
        return pltpu.make_async_remote_copy(
            src_ref=parts.at[block, pl.ds(other * quarter, quarter)],
            dst_ref=arrived.at[block, row],
            send_sem=sum_send.at[block, d],
            recv_sem=sum_recv.at[block, row],
            device_id=(sec, other, col),
            device_id_type=MESH,
        )

    def sum_wait(block, d):
        other = peer(d)
        pltpu.make_async_remote_copy(
            src_ref=arrived.at[block, other],
            dst_ref=arrived.at[block, other],
            send_sem=sum_send.at[block, d],
            recv_sem=sum_recv.at[block, other],
            device_id=(sec, other, col),
            device_id_type=MESH,
        ).wait_recv()

    def full_part(source, part):
        return full.at[pl.ds(source * units + part * quarter, quarter)]

    def full_copy(source, d):
        return pltpu.make_async_remote_copy(
            src_ref=full_part(source, row),
            dst_ref=full_part(source, row),
            send_sem=full_send.at[source, d],
            recv_sem=full_recv.at[source, row],
            device_id=(sec, peer(d), col),
            device_id_type=MESH,
        )

    def turn_copy(block):
        return pltpu.make_async_remote_copy(
            src_ref=summed.at[block],
            dst_ref=full_part(col, row),
            send_sem=turn_send.at[block],
            recv_sem=turn_recv.at[col],
            device_id=(sec, row, block),
            device_id_type=MESH,
        )

    def reduce_block(block):
        total = parts[block, pl.ds(row * quarter, quarter)].astype(F32)
        for d in range(1, n_row):
            sum_wait(block, d)
            total = total + arrived[block, peer(d)].astype(F32)
        total = total.astype(BF16)

        @pl.when(block == col)
        def _():
            full[pl.ds(col * units + row * quarter, quarter)] = total
            for d in range(1, n_row):
                full_copy(col, d).start()

        @pl.when(block != col)
        def _():
            summed[block] = total
            turn_copy(block).start()

    def step(k, carry):
        block = block_at(k)

        @pl.when(k > 0)
        def _():
            gather_copy(block, below, gather_send.at[block]).wait_recv()

        @pl.when(jnp.logical_and(block > col, col > 0))
        def _():
            gather_copy(block, below, gather_send.at[block]).start()

        @pl.when(jnp.logical_and(block < col, col < n_col - 1))
        def _():
            gather_copy(block, above, gather_send.at[block]).start()

        for t in range(tiles):
            if loads[t] is not None:

                @pl.when(k == 0)
                def _():
                    loads[t].wait()

            product = jnp.dot(gathered[block], weights[t], preferred_element_type=F32)
            product = product.astype(BF16)
            for u in range(TILE // HEAD_DIM):
                parts[block, t * (TILE // HEAD_DIM) + u] = product[
                    :, u * HEAD_DIM : (u + 1) * HEAD_DIM
                ]
        for d in range(1, n_row):
            sum_copy(block, d).start()

        @pl.when(k > 0)
        def _():
            reduce_block(block_at(k - 1))

        return carry

    lax.fori_loop(0, n_col, step, 0)
    reduce_block(block_at(n_col - 1))

    def forward(k, carry):
        source = block_at(k)
        pltpu.make_async_remote_copy(
            src_ref=full_part(source, row),
            dst_ref=full_part(source, row),
            send_sem=turn_send.at[source],
            recv_sem=turn_recv.at[source],
            device_id=(sec, row, source),
            device_id_type=MESH,
        ).wait_recv()
        for d in range(1, n_row):
            full_copy(source, d).start()
        return carry

    lax.fori_loop(1, n_col, forward, 0)

    for d in range(1, n_row):
        other = peer(d)
        pltpu.make_async_remote_copy(
            src_ref=squares.at[other],
            dst_ref=squares.at[other],
            send_sem=square_send.at[d],
            recv_sem=square_recv.at[other],
            device_id=(sec, other, col),
            device_id_type=MESH,
        ).wait_recv()
    square_sum = squares[0]
    for i in range(1, n_row):
        square_sum = square_sum + squares[i]
    scaling = lax.rsqrt(square_sum / (width * n_row) + EPSILON)
    cache_load.wait()

    def head_unit(head):
        return (head // heads_per) * units + head % heads_per

    def pair_unit(pair):
        return (pair // pairs_per) * units + heads_per + pair % pairs_per

    def scaled(unit, p):
        some = pl.ds(p * samples, samples)
        factor = scaling[p * samples : (p + 1) * samples]
        return (full[unit, some, :].astype(F32) * factor).astype(BF16)

    def queries(g, p):
        return jnp.concatenate([scaled(head_unit(g * group + i), p) for i in range(group)], axis=0)

    score_scale = HEAD_DIM ** (-0.5)
    lane = lax.broadcasted_iota(jnp.int32, (tall, HEAD_DIM), 1)
    spot = lax.broadcasted_iota(jnp.int32, (1, slots), 1)
    position = row * (slots // 2) + spot // 2
    is_key = spot % 2 == 0

    def attend(g, p):
        q = queries(g, p)
        both = cache[p, :, pl.ds(pl.multiple_of(g * HEAD_DIM, HEAD_DIM), HEAD_DIM)]
        scores = (
            lax.dot_general(q, both, (((1,), (1,)), ((), ())), preferred_element_type=F32)
            * score_scale
        )
        valid = jnp.logical_and(is_key, position < len_ref[0, p])
        scores = jnp.where(valid, scores, FLOOR)
        top = jnp.max(scores, axis=1, keepdims=True)
        weight = jnp.where(valid, jnp.exp(scores - top), 0.0)
        total = jnp.sum(weight, axis=1, keepdims=True)
        moved = pltpu.roll(weight, 1, 1).astype(BF16)
        out = jnp.dot(moved, both, preferred_element_type=F32)
        outs[g, p] = out.astype(BF16)
        at = (g * prompts + p) * 2
        tile = jnp.where(lane == at, top, stat_tile[...])
        stat_tile[...] = jnp.where(lane == at + 1, total, tile)

    def out_copy(dest):
        return pltpu.make_async_remote_copy(
            src_ref=outs.at[pl.ds(dest * mine, mine)],
            dst_ref=outs_in.at[row],
            send_sem=out_send.at[dest],
            recv_sem=out_recv.at[row],
            device_id=(sec, dest, col),
            device_id_type=MESH,
        )

    chunk_heads = max(1, heads_per // group)
    chunk_cols = max(1, group // heads_per)
    chunks = kv_heads // chunk_heads
    stat_tile[...] = jnp.zeros_like(stat_tile)

    def chunk(k, carry):
        j = block_at(k) if chunk_cols == 1 and chunks == n_col else k
        for i in range(chunk_cols):
            source = j * chunk_cols + i
            for d in range(1, n_row):
                other = peer(d)
                pltpu.make_async_remote_copy(
                    src_ref=full_part(source, other),
                    dst_ref=full_part(source, other),
                    send_sem=full_send.at[source, d],
                    recv_sem=full_recv.at[source, other],
                    device_id=(sec, other, col),
                    device_id_type=MESH,
                ).wait_recv()
        for i in range(chunk_heads):
            g = j * chunk_heads + i
            for p in range(prompts):
                attend(g, p)
            dest = g // mine

            @pl.when(jnp.logical_and(g % mine == mine - 1, dest != row))
            def _():
                out_copy(dest).start()

        return carry

    lax.fori_loop(0, chunks, chunk, 0)

    stat_rows[...] = stat_tile[...].T
    per_dest = mine * prompts * 2

    def stat_copy(d):
        other = peer(d)
        return pltpu.make_async_remote_copy(
            src_ref=stat_rows.at[pl.ds(pl.multiple_of(other * per_dest, per_dest), per_dest)],
            dst_ref=stat_in.at[pl.ds(pl.multiple_of(row * per_dest, per_dest), per_dest)],
            send_sem=stat_send.at[d],
            recv_sem=stat_recv.at[row],
            device_id=(sec, other, col),
            device_id_type=MESH,
        )

    for d in range(1, n_row):
        stat_copy(d).start()

    stat_in[n_row * per_dest :] = jnp.zeros((HEAD_DIM - n_row * per_dest, tall), F32)
    here = pl.ds(pl.multiple_of(row * per_dest, per_dest), per_dest)
    stat_in[here] = stat_rows[here]
    outs_in[row] = outs[pl.ds(row * mine, mine)]

    for pair in range(2 * kv_heads):
        newkv_ref[:, pair * HEAD_DIM : (pair + 1) * HEAD_DIM] = (
            full[pair_unit(pair)].astype(F32) * scaling
        ).astype(BF16)

    for d in range(1, n_row):
        other = peer(d)
        landed = pl.ds(pl.multiple_of(other * per_dest, per_dest), per_dest)
        pltpu.make_async_remote_copy(
            src_ref=stat_in.at[landed],
            dst_ref=stat_in.at[landed],
            send_sem=stat_send.at[d],
            recv_sem=stat_recv.at[other],
            device_id=(sec, other, col),
            device_id_type=MESH,
        ).wait_recv()
        pltpu.make_async_remote_copy(
            src_ref=outs_in.at[other],
            dst_ref=outs_in.at[other],
            send_sem=out_send.at[other],
            recv_sem=out_recv.at[other],
            device_id=(sec, other, col),
            device_id_type=MESH,
        ).wait_recv()

    stats = stat_in[...].T
    for i in range(mine):
        g = row * mine + i
        for p in range(prompts):
            q = queries(g, p).astype(F32)
            new_key = jnp.concatenate([scaled(pair_unit(g), p)] * group, axis=0)
            new_value = jnp.concatenate([scaled(pair_unit(kv_heads + g), p)] * group, axis=0)
            own = jnp.sum(q * new_key.astype(F32), axis=1, keepdims=True) * score_scale
            top = own
            tops, totals = [], []
            for s in range(n_row):
                at = s * per_dest + (i * prompts + p) * 2
                tops.append(stats[:, at : at + 1])
                totals.append(stats[:, at + 1 : at + 2])
                top = jnp.maximum(top, tops[-1])
            own_weight = jnp.exp(own - top)
            total = own_weight
            value = own_weight.astype(BF16).astype(F32) * new_value.astype(F32)
            for s in range(n_row):
                keep = jnp.exp(tops[s] - top)
                total = total + keep * totals[s]
                value = value + keep * outs_in[s, i, p].astype(F32)
            done = (value / total).astype(BF16)
            for h in range(group):
                first = (i * group + h) * HEAD_DIM
                final[p * samples : (p + 1) * samples, first : first + HEAD_DIM] = done[
                    h * samples : (h + 1) * samples
                ]

    hand = pltpu.make_async_remote_copy(
        src_ref=final,
        dst_ref=handed_ref,
        send_sem=hand_send,
        recv_sem=hand_recv,
        device_id=(lax.rem(sec + 1, n_sec), row, col),
        device_id_type=MESH,
    )
    hand.start()

    @pl.when(col > 0)
    def _():
        gather_copy(col, below, gather_send.at[col]).wait_send()

    @pl.when(col < n_col - 1)
    def _():
        gather_copy(col, above, own_send).wait_send()

    def drain(k, carry):
        block = block_at(k)

        @pl.when(
            jnp.logical_or(
                jnp.logical_and(block > col, col > 0),
                jnp.logical_and(block < col, col < n_col - 1),
            )
        )
        def _():
            gather_copy(block, below, gather_send.at[block]).wait_send()

        @pl.when(block != col)
        def _():
            turn_copy(block).wait_send()

        for d in range(1, n_row):
            sum_copy(block, d).wait_send()
            full_copy(block, d).wait_send()
        return carry

    lax.fori_loop(0, n_col, drain, 0)
    for d in range(1, n_row):
        square_copy(d).wait_send()
        stat_copy(d).wait_send()
        out_copy(peer(d)).wait_send()
    hand.wait()


def shards(n_sec, n_row, n_col, hidden_in, norm_gain, q_weight, kv_weight, kv_cache, lengths):
    _, rows, width = hidden_in.shape
    _, prompts, positions, _, cache_width = kv_cache.shape
    kv_heads = cache_width // HEAD_DIM
    heads_per = q_weight.shape[2] // HEAD_DIM
    pairs_per = kv_weight.shape[2] // HEAD_DIM
    units = -(-(heads_per + pairs_per) // 4) * 4
    quarter = units // n_row
    group = heads_per * n_col // kv_heads
    tall = group * (rows // prompts)
    mine = kv_heads // n_row
    tiles = units * HEAD_DIM // TILE
    dims = (n_sec, n_row, n_col, units, quarter, heads_per, pairs_per, kv_heads)
    dma = pltpu.SemaphoreType.DMA
    vmem = pl.BlockSpec(memory_space=pltpu.VMEM)
    anywhere = pl.BlockSpec(memory_space=pl.ANY)
    handed, new_kv = pl.pallas_call(
        functools.partial(kernel, dims),
        out_shape=(
            jax.ShapeDtypeStruct((rows, heads_per * n_col // n_row * HEAD_DIM), BF16),
            jax.ShapeDtypeStruct((rows, 2 * cache_width), BF16),
        ),
        in_specs=[
            vmem,
            vmem,
            anywhere,
            anywhere,
            anywhere,
            pl.BlockSpec(memory_space=pltpu.SMEM),
        ],
        out_specs=(vmem, vmem),
        scratch_shapes=[
            pltpu.VMEM((tiles, width, TILE), BF16),
            pltpu.VMEM((prompts, 2 * positions, cache_width), BF16),
            pltpu.VMEM((n_col, rows, width), BF16),
            pltpu.VMEM((n_col, units, rows, HEAD_DIM), BF16),
            pltpu.VMEM((n_col, n_row, quarter, rows, HEAD_DIM), BF16),
            pltpu.VMEM((n_col, quarter, rows, HEAD_DIM), BF16),
            pltpu.VMEM((n_col * units, rows, HEAD_DIM), BF16),
            pltpu.VMEM((kv_heads, prompts, tall, HEAD_DIM), BF16),
            pltpu.VMEM((n_row, mine, prompts, tall, HEAD_DIM), BF16),
            pltpu.VMEM((tall, HEAD_DIM), F32),
            pltpu.VMEM((HEAD_DIM, tall), F32),
            pltpu.VMEM((HEAD_DIM, tall), F32),
            pltpu.VMEM((n_row, rows, HEAD_DIM), F32),
            pltpu.VMEM((rows, heads_per * n_col // n_row * HEAD_DIM), BF16),
            dma((tiles,)),
            dma,
            dma((n_col,)),
            dma((n_col,)),
            dma,
            dma((n_col, n_row)),
            dma((n_col, n_row)),
            dma((n_col,)),
            dma((n_col,)),
            dma((n_col, n_row)),
            dma((n_col, n_row)),
            dma((n_row,)),
            dma((n_row,)),
            dma((n_row,)),
            dma((n_row,)),
            dma((n_row,)),
            dma((n_row,)),
            dma,
            dma,
        ],
        compiler_params=pltpu.CompilerParams(
            collective_id=0, has_side_effects=True, vmem_limit_bytes=48 * 1024 * 1024
        ),
    )(
        hidden_in[0],
        norm_gain,
        q_weight[0],
        kv_weight[0],
        kv_cache[0].reshape(prompts, 2 * positions, cache_width),
        lengths,
    )
    return handed[None], new_kv[None]


def solution(mesh):
    n_sec, n_row, n_col = (mesh.shape[name] for name in ("section", "row", "col"))
    return jax.shard_map(
        functools.partial(shards, n_sec, n_row, n_col),
        mesh=mesh,
        in_specs=(
            P("section", "col", "row"),
            P("section", "row"),
            P("section", "row", "col"),
            P("section", "row", "col"),
            P("section", "col", "row", None, None),
            P("section", "col"),
        ),
        out_specs=(P("section", "col", "row"), P("section", "col", None)),
        check_vma=False,
    )
```

time: 145 us -> 57.6 us (0.40); the launches traced: 143 us -> 57.4 us
  blocking collectives: 59.4 us -> 0 us
  Pallas kernels: 0 us -> 51 us
  waiting for transfers between devices: 15.6 us -> 0 us
  local copies, waits for them, and re-layouts: 21.3 us -> 5.72 us
  between operations: 14.2 us -> 0.7 us
  other arithmetic: 13.1 us -> 0 us
  starting transfers between devices: 11.2 us -> 0 us
  matrix products: 7.82 us -> 0 us
    pallas_call x0 -> x1, Pallas kernels: none -> 51 us  [shards(): pl.pallas_call(functools.partial(kernel, dims), out_shape=(jax.ShapeDtype...]
    psum x2 -> x0, blocking collectives: 32.9 us -> none  [the longest x1 27.1 us: shards(): query_total, pair_total = lax.psum((query_part, pair_part), 'row')]
    all_gather x3 -> x0, blocking collectives: 26.5 us -> none  [the longest x1 16 us: shards(): lax.all_gather(normed.reshape(row_count, sub_rows, width_part), 'col', ax...]
    all_to_all x2 -> x0, waiting for transfers between devices: 12.1 us -> none  [the longest x1 6.24 us: shards(): lax.all_to_all(query_blocks, 'col', split_axis=1, concat_axis=3, tiled=True)]
    all_to_all x2 -> x0, starting transfers between devices: 9.6 us -> none  [the longest x1 6.27 us: shards(): lax.all_to_all(query_blocks, 'col', split_axis=1, concat_axis=3, tiled=True)]
    dot_general x5 -> x0, matrix products: 7.82 us -> none  [the longest x1 4.66 us: shards(): jnp.dot(flat_rows, query_weight, preferred_element_type=jnp.float32)]
    add x8 -> x0, other arithmetic: 6.09 us -> none  [the longest x3 6 us: join_parts(): former[2] * keep_former[..., None] + latter[2] * keep_latter[..., None]]
    unnamed x15 -> x10, local copies, waits for them, and re-layouts: 7.49 us -> 2.91 us
  transfers between devices with their start and end apart: 4 -> 0, of which waited for: 3 -> 0; matrix products, arithmetic and copies ran while one was open for 10% -> 0% of each run, Pallas kernels for 0% -> 0%
where the time goes in v1:
time: 57.6 us; the launch traced here: 57.4 us
  Pallas kernels  51 us (89%)
  local copies, waits for them, and re-layouts  5.72 us (10%)
  between operations  0.7 us (1%)
    pallas_call x1, Pallas kernels, shards(): pl.pallas_call(functools.partial(kernel, dims), out_shape=(jax.ShapeDtype...  51 us
    unnamed x10, local copies, waits for them, and re-layouts  2.91 us
    another operation x1, local copies, waits for them, and re-layouts, shards(): kv_cache[0].reshape(prompts, 2 * positions, cache_width)  2.81 us

profile of v1, /device:TPU:2, one launch (start us, length us, event | category | flops | bytes accessed | tf_op | source)
XLA Modules:
  0.0 57.4 jit_solution(5914451913996941063)
XLA Ops:
  0.6 0.0 copy-start.1
  0.6 0.0 copy-start.2
  0.7 0.0 copy-start.3
  0.7 2.8 %reshape_squeeze.3.cache_ref = bf16[2,512,1024]{2,1,0:T(8,128)(2,1)S(1)} reshape(bf16[1,2,256,2,1024]{4,3,2,1,0:T(2,128)(2,1)} %param.10) | data formatting | bytes 4194304 | tf_op jit(solution)/shard_map/reshape;squeeze | solution.py:584
  3.5 0.0 copy-done.1
  3.5 0.0 copy-done.2
  3.5 0.0 copy-done.3
  3.5 0.0 copy-start
  3.5 1.6 %copy-done = bf16[1,2048,512]{2,1,0:T(8,128)(2,1)S(1)} copy-done((bf16[1,2048,512]{2,1,0:T(8,128)(2,1)S(1)}, bf16[1,2048,512]{2,1,0:T(8,128)(2,1)}, u32[]{:S(2)}) %copy-start) | copy-done | bytes 2097176
  5.1 51.0 %shard_map.77 = (bf16[32,2048]{1,0:T(8,128)(2,1)S(1)}, bf16[32,2048]{1,0:T(8,128)(2,1)S(1)}) custom-call(bf16[32,2048]{1,0:T(8,128)(2,1)S(1)} %bitcast.6, f32[1,2048]{1,0:T(1,128)S(1)} %copy-done.2, bf16[2048,2048]{1,0:T(8,128)(2,1)} %bitcast.9, bf16[2048,512]{1,0:T(8,128)(2,1)S(1)} %bitcast.5, bf16[2,512,1024]{2,1,0:T(8,128)(2,1)S(1)} %reshape_squeeze.3.cache_ref, ...), custom_call_target="tpu_custom_call" | custom-call | tf_op jit(solution)/shard_map/pallas_call | solution.py:526
  56.1 0.7 %copy.10 = bf16[1,32,2048]{2,1,0:T(8,128)(2,1)} copy(bf16[1,32,2048]{2,1,0:T(8,128)(2,1)S(1)} %bitcast.8) | data formatting | bytes 262144
  56.7 0.7 %copy.11 = bf16[1,32,2048]{2,1,0:T(8,128)(2,1)} copy(bf16[1,32,2048]{2,1,0:T(8,128)(2,1)S(1)} %bitcast.7) | data formatting | bytes 262144
Async XLA Ops:
  0.6 2.9 %copy-start.1 = (bf16[1,32,2048]{2,1,0:T(8,128)(2,1)S(1)}, bf16[1,32,2048]{2,1,0:T(8,128)(2,1)}, u32[]{:S(2)}) copy-start(bf16[1,32,2048]{2,1,0:T(8,128)(2,1)} %param.6) | copy-start | bytes 393220
  0.6 2.9 %copy-start.2 = (f32[1,2048]{1,0:T(1,128)S(1)}, f32[1,2048]{1,0:T(1,128)}, u32[]{:S(2)}) copy-start(f32[1,2048]{1,0:T(1,128)} %gain_ref.1) | copy-start | bytes 24580
  0.7 2.9 %copy-start.3 = (s32[1,2]{1,0:T(1,128)S(1)}, s32[1,2]{1,0:T(1,128)}, u32[]{:S(2)}) copy-start(s32[1,2]{1,0:T(1,128)} %len_ref.1) | copy-start | bytes 28
  3.5 1.6 %copy-start = (bf16[1,2048,512]{2,1,0:T(8,128)(2,1)S(1)}, bf16[1,2048,512]{2,1,0:T(8,128)(2,1)}, u32[]{:S(2)}) copy-start(bf16[1,2048,512]{2,1,0:T(8,128)(2,1)} %param.9) | copy-start | bytes 6291460

commit v2 on v1

--- a/solution.py
+++ b/solution.py
@@ -28,6 +28,8 @@
     newkv_ref,
     weights,
     cache,
+    keys,
+    values,
     gathered,
     parts,
     arrived,
@@ -35,7 +37,6 @@
     full,
     outs,
     outs_in,
-    stat_tile,
     stat_rows,
     stat_in,
     squares,
@@ -63,7 +64,7 @@
     n_sec, n_row, n_col, units, quarter, heads_per, pairs_per, kv_heads = dims
     sec, row, col = lax.axis_index("section"), lax.axis_index("row"), lax.axis_index("col")
     rows, width = hidden_ref.shape
-    prompts, slots = cache_ref.shape[0], cache_ref.shape[1]
+    prompts, positions = cache_ref.shape[0], cache_ref.shape[1]
     samples = rows // prompts
     group = (heads_per * n_col) // kv_heads
     tall = group * samples
@@ -71,6 +72,10 @@
     q_tiles = qw_ref.shape[1] // TILE
     tiles = units * HEAD_DIM // TILE
     pair_cols = kvw_ref.shape[1]
+
+    mate = row + 1 - 2 * (row % 2)
+    across = (row + 2) % 4
+    far_peer = (mate + 2) % 4
 
     def peer(d):
         return lax.rem(row + d, n_row)
@@ -95,11 +100,11 @@
             )
         else:
             loads.append(None)
+    cache_load = pltpu.make_async_copy(cache_ref, cache, cache_sem)
+    cache_load.start()
     for load in loads:
         if load is not None:
             load.start()
-    cache_load = pltpu.make_async_copy(cache_ref, cache, cache_sem)
-    cache_load.start()
 
     barrier = pltpu.get_barrier_semaphore()
     for d in range(1, n_row):
@@ -158,6 +163,26 @@
     for d in range(1, n_row):
         square_copy(d).start()
 
+    slots = 2 * positions
+    picked = lax.broadcasted_iota(jnp.int32, (slots, slots), 0)
+    offered = lax.broadcasted_iota(jnp.int32, (slots, slots), 1)
+    wanted = jnp.where(picked < positions, 2 * picked, 2 * (picked - positions) + 1)
+    pick = jnp.where(offered == wanted, 1.0, 0.0).astype(BF16)
+    cache_load.wait()
+    strip = 2 * HEAD_DIM
+    strips = cache_ref.shape[3] // strip
+
+    def split(k, carry):
+        p = k // strips
+        some = pl.ds(pl.multiple_of((k % strips) * strip, strip), strip)
+        both = cache[p, :, :, some].reshape(slots, strip)
+        apart = jnp.dot(pick, both, preferred_element_type=F32).astype(BF16)
+        keys[p, :, some] = apart[:positions]
+        values[p, :, some] = apart[positions:]
+        return carry
+
+    lax.fori_loop(0, prompts * strips, split, 0)
+
     shorter = jnp.minimum(col, n_col - 1 - col)
     upward = col < n_col - 1 - col
 
@@ -192,15 +217,23 @@
     def full_part(source, part):
         return full.at[pl.ds(source * units + part * quarter, quarter)]
 
-    def full_copy(source, d):
-        return pltpu.make_async_remote_copy(
-            src_ref=full_part(source, row),
-            dst_ref=full_part(source, row),
-            send_sem=full_send.at[source, d],
-            recv_sem=full_recv.at[source, row],
-            device_id=(sec, peer(d), col),
-            device_id_type=MESH,
-        )
+    def full_copy(source, part, to, sem):
+        return pltpu.make_async_remote_copy(
+            src_ref=full_part(source, part),
+            dst_ref=full_part(source, part),
+            send_sem=full_send.at[source, sem],
+            recv_sem=full_recv.at[source, part],
+            device_id=(sec, to, col),
+            device_id_type=MESH,
+        )
+
+    def spread(source):
+        full_copy(source, row, across, 0).start()
+        full_copy(source, row, mate, 1).start()
+
+    def relay(source):
+        full_copy(source, across, mate, 2).wait_recv()
+        full_copy(source, across, mate, 2).start()
 
     def turn_copy(block):
         return pltpu.make_async_remote_copy(
@@ -222,8 +255,7 @@
         @pl.when(block == col)
         def _():
             full[pl.ds(col * units + row * quarter, quarter)] = total
-            for d in range(1, n_row):
-                full_copy(col, d).start()
+            spread(col)
 
         @pl.when(block != col)
         def _():
@@ -280,11 +312,12 @@
             device_id=(sec, row, source),
             device_id_type=MESH,
         ).wait_recv()
-        for d in range(1, n_row):
-            full_copy(source, d).start()
+        spread(source)
+        relay(block_at(k - 1))
         return carry
 
     lax.fori_loop(1, n_col, forward, 0)
+    relay(block_at(n_col - 1))
 
     for d in range(1, n_row):
         other = peer(d)
@@ -300,7 +333,6 @@
     for i in range(1, n_row):
         square_sum = square_sum + squares[i]
     scaling = lax.rsqrt(square_sum / (width * n_row) + EPSILON)
-    cache_load.wait()
 
     def head_unit(head):
         return (head // heads_per) * units + head % heads_per
@@ -318,28 +350,46 @@
 
     score_scale = HEAD_DIM ** (-0.5)
     lane = lax.broadcasted_iota(jnp.int32, (tall, HEAD_DIM), 1)
-    spot = lax.broadcasted_iota(jnp.int32, (1, slots), 1)
-    position = row * (slots // 2) + spot // 2
-    is_key = spot % 2 == 0
-
-    def attend(g, p):
-        q = queries(g, p)
-        both = cache[p, :, pl.ds(pl.multiple_of(g * HEAD_DIM, HEAD_DIM), HEAD_DIM)]
-        scores = (
-            lax.dot_general(q, both, (((1,), (1,)), ((), ())), preferred_element_type=F32)
-            * score_scale
-        )
-        valid = jnp.logical_and(is_key, position < len_ref[0, p])
-        scores = jnp.where(valid, scores, FLOOR)
-        top = jnp.max(scores, axis=1, keepdims=True)
-        weight = jnp.where(valid, jnp.exp(scores - top), 0.0)
-        total = jnp.sum(weight, axis=1, keepdims=True)
-        moved = pltpu.roll(weight, 1, 1).astype(BF16)
-        out = jnp.dot(moved, both, preferred_element_type=F32)
-        outs[g, p] = out.astype(BF16)
-        at = (g * prompts + p) * 2
-        tile = jnp.where(lane == at, top, stat_tile[...])
-        stat_tile[...] = jnp.where(lane == at + 1, total, tile)
+    position = row * positions + lax.broadcasted_iota(jnp.int32, (1, positions), 1)
+    valid = [position < len_ref[0, p] for p in range(prompts)]
+
+    def attend(heads):
+        pairs = [(g, p) for g in heads for p in range(prompts)]
+
+        def some(g):
+            return pl.ds(pl.multiple_of(g * HEAD_DIM, HEAD_DIM), HEAD_DIM)
+
+        scores = [
+            lax.dot_general(
+                queries(g, p),
+                keys[p, :, some(g)],
+                (((1,), (1,)), ((), ())),
+                preferred_element_type=F32,
+            )
+            for g, p in pairs
+        ]
+        scores = [
+            jnp.where(valid[p], score * score_scale, FLOOR)
+            for (g, p), score in zip(pairs, scores)
+        ]
+        tops = [jnp.max(score, axis=1, keepdims=True) for score in scores]
+        raised = [
+            jnp.where(valid[p], jnp.exp(score - top), 0.0)
+            for (g, p), score, top in zip(pairs, scores, tops)
+        ]
+        totals = [jnp.sum(weight, axis=1, keepdims=True) for weight in raised]
+        products = [
+            jnp.dot(weight.astype(BF16), values[p, :, some(g)], preferred_element_type=F32)
+            for (g, p), weight in zip(pairs, raised)
+        ]
+        for (g, p), product in zip(pairs, products):
+            outs[g, p] = product.astype(BF16)
+        for i, g in enumerate(heads):
+            tile = jnp.zeros((tall, HEAD_DIM), F32)
+            for p in range(prompts):
+                tile = jnp.where(lane == 2 * p, tops[i * prompts + p], tile)
+                tile = jnp.where(lane == 2 * p + 1, totals[i * prompts + p], tile)
+            stat_rows[g] = tile.T[:8]
 
     def out_copy(dest):
         return pltpu.make_async_remote_copy(
@@ -354,70 +404,60 @@
     chunk_heads = max(1, heads_per // group)
     chunk_cols = max(1, group // heads_per)
     chunks = kv_heads // chunk_heads
-    stat_tile[...] = jnp.zeros_like(stat_tile)
+    by_dest = chunks == n_row and chunk_heads == mine
+
+    def stat_copy(dest):
+        return pltpu.make_async_remote_copy(
+            src_ref=stat_rows.at[pl.ds(dest * mine, mine)],
+            dst_ref=stat_in.at[row],
+            send_sem=stat_send.at[dest],
+            recv_sem=stat_recv.at[row],
+            device_id=(sec, dest, col),
+            device_id_type=MESH,
+        )
 
     def chunk(k, carry):
-        j = block_at(k) if chunk_cols == 1 and chunks == n_col else k
+        j = k
+        if by_dest:
+            j = jnp.where(k == 0, across, jnp.where(k == 1, far_peer, jnp.where(k == 2, mate, row)))
         for i in range(chunk_cols):
             source = j * chunk_cols + i
-            for d in range(1, n_row):
-                other = peer(d)
-                pltpu.make_async_remote_copy(
-                    src_ref=full_part(source, other),
-                    dst_ref=full_part(source, other),
-                    send_sem=full_send.at[source, d],
-                    recv_sem=full_recv.at[source, other],
-                    device_id=(sec, other, col),
-                    device_id_type=MESH,
-                ).wait_recv()
-        for i in range(chunk_heads):
-            g = j * chunk_heads + i
-            for p in range(prompts):
-                attend(g, p)
-            dest = g // mine
-
-            @pl.when(jnp.logical_and(g % mine == mine - 1, dest != row))
-            def _():
-                out_copy(dest).start()
+            full_copy(source, mate, mate, 1).wait_recv()
+            full_copy(source, far_peer, mate, 2).wait_recv()
+        attend([j * chunk_heads + i for i in range(chunk_heads)])
+        last = j * chunk_heads + chunk_heads - 1
+        dest = last // mine
+
+        @pl.when(jnp.logical_and(last % mine == mine - 1, dest != row))
+        def _():
+            out_copy(dest).start()
+            stat_copy(dest).start()
 
         return carry
 
     lax.fori_loop(0, chunks, chunk, 0)
 
-    stat_rows[...] = stat_tile[...].T
-    per_dest = mine * prompts * 2
-
-    def stat_copy(d):
-        other = peer(d)
-        return pltpu.make_async_remote_copy(
-            src_ref=stat_rows.at[pl.ds(pl.multiple_of(other * per_dest, per_dest), per_dest)],
-            dst_ref=stat_in.at[pl.ds(pl.multiple_of(row * per_dest, per_dest), per_dest)],
-            send_sem=stat_send.at[d],
-            recv_sem=stat_recv.at[row],
-            device_id=(sec, other, col),
-            device_id_type=MESH,
-        )
-
-    for d in range(1, n_row):
-        stat_copy(d).start()
-
-    stat_in[n_row * per_dest :] = jnp.zeros((HEAD_DIM - n_row * per_dest, tall), F32)
-    here = pl.ds(pl.multiple_of(row * per_dest, per_dest), per_dest)
-    stat_in[here] = stat_rows[here]
     outs_in[row] = outs[pl.ds(row * mine, mine)]
+    stat_in[row] = stat_rows[pl.ds(row * mine, mine)]
 
     for pair in range(2 * kv_heads):
         newkv_ref[:, pair * HEAD_DIM : (pair + 1) * HEAD_DIM] = (
             full[pair_unit(pair)].astype(F32) * scaling
         ).astype(BF16)
 
+    def own_part(g, p):
+        new_key = jnp.concatenate([scaled(pair_unit(g), p)] * group, axis=0)
+        product = queries(g, p).astype(F32) * new_key.astype(F32)
+        return jnp.sum(product, axis=1, keepdims=True) * score_scale
+
+    own_scores = [[own_part(row * mine + i, p) for p in range(prompts)] for i in range(mine)]
+
     for d in range(1, n_row):
         other = peer(d)
-        landed = pl.ds(pl.multiple_of(other * per_dest, per_dest), per_dest)
         pltpu.make_async_remote_copy(
-            src_ref=stat_in.at[landed],
-            dst_ref=stat_in.at[landed],
-            send_sem=stat_send.at[d],
+            src_ref=stat_in.at[other],
+            dst_ref=stat_in.at[other],
+            send_sem=stat_send.at[other],
             recv_sem=stat_recv.at[other],
             device_id=(sec, other, col),
             device_id_type=MESH,
@@ -431,18 +471,29 @@
             device_id_type=MESH,
         ).wait_recv()
 
-    stats = stat_in[...].T
+    lines = stat_in[...].reshape(n_row * mine * 8, tall)
+    stats = jnp.concatenate([lines, jnp.zeros((HEAD_DIM - n_row * mine * 8, tall), F32)], axis=0).T
+    span = group * HEAD_DIM
+
+    def hand_copy(i):
+        return pltpu.make_async_remote_copy(
+            src_ref=final.at[:, pl.ds(i * span, span)],
+            dst_ref=handed_ref.at[:, pl.ds(i * span, span)],
+            send_sem=hand_send.at[i],
+            recv_sem=hand_recv.at[i],
+            device_id=(lax.rem(sec + 1, n_sec), row, col),
+            device_id_type=MESH,
+        )
+
     for i in range(mine):
         g = row * mine + i
         for p in range(prompts):
-            q = queries(g, p).astype(F32)
-            new_key = jnp.concatenate([scaled(pair_unit(g), p)] * group, axis=0)
             new_value = jnp.concatenate([scaled(pair_unit(kv_heads + g), p)] * group, axis=0)
-            own = jnp.sum(q * new_key.astype(F32), axis=1, keepdims=True) * score_scale
+            own = own_scores[i][p]
             top = own
             tops, totals = [], []
             for s in range(n_row):
-                at = s * per_dest + (i * prompts + p) * 2
+                at = (s * mine + i) * 8 + 2 * p
                 tops.append(stats[:, at : at + 1])
                 totals.append(stats[:, at + 1 : at + 2])
                 top = jnp.maximum(top, tops[-1])
@@ -459,16 +510,7 @@
                 final[p * samples : (p + 1) * samples, first : first + HEAD_DIM] = done[
                     h * samples : (h + 1) * samples
                 ]
-
-    hand = pltpu.make_async_remote_copy(
-        src_ref=final,
-        dst_ref=handed_ref,
-        send_sem=hand_send,
-        recv_sem=hand_recv,
-        device_id=(lax.rem(sec + 1, n_sec), row, col),
-        device_id_type=MESH,
-    )
-    hand.start()
+        hand_copy(i).start()
 
     @pl.when(col > 0)
     def _():
@@ -496,15 +538,18 @@
 
         for d in range(1, n_row):
             sum_copy(block, d).wait_send()
-            full_copy(block, d).wait_send()
+        full_copy(block, row, across, 0).wait_send()
+        full_copy(block, row, mate, 1).wait_send()
+        full_copy(block, across, mate, 2).wait_send()
         return carry
 
     lax.fori_loop(0, n_col, drain, 0)
     for d in range(1, n_row):
         square_copy(d).wait_send()
-        stat_copy(d).wait_send()
+        stat_copy(peer(d)).wait_send()
         out_copy(peer(d)).wait_send()
-    hand.wait()
+    for i in range(mine):
+        hand_copy(i).wait()
 
 
 def shards(n_sec, n_row, n_col, hidden_in, norm_gain, q_weight, kv_weight, kv_cache, lengths):
@@ -540,7 +585,9 @@
         out_specs=(vmem, vmem),
         scratch_shapes=[
             pltpu.VMEM((tiles, width, TILE), BF16),
-            pltpu.VMEM((prompts, 2 * positions, cache_width), BF16),
+            pltpu.VMEM((prompts, positions, 2, cache_width), BF16),
+            pltpu.VMEM((prompts, positions, cache_width), BF16),
+            pltpu.VMEM((prompts, positions, cache_width), BF16),
             pltpu.VMEM((n_col, rows, width), BF16),
             pltpu.VMEM((n_col, units, rows, HEAD_DIM), BF16),
             pltpu.VMEM((n_col, n_row, quarter, rows, HEAD_DIM), BF16),
@@ -548,9 +595,8 @@
             pltpu.VMEM((n_col * units, rows, HEAD_DIM), BF16),
             pltpu.VMEM((kv_heads, prompts, tall, HEAD_DIM), BF16),
             pltpu.VMEM((n_row, mine, prompts, tall, HEAD_DIM), BF16),
-            pltpu.VMEM((tall, HEAD_DIM), F32),
-            pltpu.VMEM((HEAD_DIM, tall), F32),
-            pltpu.VMEM((HEAD_DIM, tall), F32),
+            pltpu.VMEM((kv_heads, 8, tall), F32),
+            pltpu.VMEM((n_row, mine, 8, tall), F32),
             pltpu.VMEM((n_row, rows, HEAD_DIM), F32),
             pltpu.VMEM((rows, heads_per * n_col // n_row * HEAD_DIM), BF16),
             dma((tiles,)),
@@ -570,18 +616,18 @@
             dma((n_row,)),
             dma((n_row,)),
             dma((n_row,)),
-            dma,
-            dma,
+            dma((mine,)),
+            dma((mine,)),
         ],
         compiler_params=pltpu.CompilerParams(
-            collective_id=0, has_side_effects=True, vmem_limit_bytes=48 * 1024 * 1024
+            collective_id=0, has_side_effects=True, vmem_limit_bytes=60 * 1024 * 1024
         ),
     )(
         hidden_in[0],
         norm_gain,
         q_weight[0],
         kv_weight[0],
-        kv_cache[0].reshape(prompts, 2 * positions, cache_width),
+        kv_cache[0],
         lengths,
     )
     return handed[None], new_kv[None]

time: 57.6 us -> 56.6 us (0.983)
  local copies, waits for them, and re-layouts: 5.72 us -> 3.14 us
  Pallas kernels: 51 us -> 52.6 us
    another operation x1 -> x0, local copies, waits for them, and re-layouts: 2.81 us -> none  [shards(): kv_cache[0].reshape(prompts, 2 * positions, cache_width)]
    pallas_call x1, Pallas kernels: 51 us -> 52.6 us  [shards(): pl.pallas_call(functools.partial(kernel, dims), out_shape=(jax.ShapeDtype...]
    unnamed x10 -> x2, local copies, waits for them, and re-layouts: 2.91 us -> 3.14 us
where the time goes in v2:
time: 56.6 us; the launch traced here: 56.4 us
  Pallas kernels  52.6 us (93%)
  local copies, waits for them, and re-layouts  3.14 us (6%)
  between operations  0.64 us (1%)
    pallas_call x1, Pallas kernels, shards(): pl.pallas_call(functools.partial(kernel, dims), out_shape=(jax.ShapeDtype...  52.6 us
    unnamed x2, local copies, waits for them, and re-layouts  3.14 us

profile of v2, /device:TPU:2, one launch (start us, length us, event | category | flops | bytes accessed | tf_op | source)
XLA Modules:
  0.0 56.4 jit_solution(9362171983920425553)
XLA Ops:
  0.6 52.6 %shard_map.77 = (bf16[32,2048]{1,0:T(8,128)(2,1)}, bf16[32,2048]{1,0:T(8,128)(2,1)}) custom-call(bf16[32,2048]{1,0:T(8,128)(2,1)} %bitcast.9, f32[1,2048]{1,0:T(1,128)} %gain_ref.1, bf16[2048,2048]{1,0:T(8,128)(2,1)} %bitcast.6, bf16[2048,512]{1,0:T(8,128)(2,1)} %bitcast.7, bf16[2,256,2,1024]{3,2,1,0:T(2,128)(2,1)} %bitcast.8, s32[1,2]{1,0:T(1,128)} %len_ref.1), custom_call_target="tpu_custom_call" | custom-call | tf_op jit(solution)/shard_map/pallas_call | solution.py:571
  53.3 1.6 %copy.10 = bf16[1,32,2048]{2,1,0:T(8,128)(2,1)} copy(bf16[1,32,2048]{2,1,0:T(8,128)(2,1)} %bitcast.11) | data formatting | bytes 262144
  54.9 1.6 %copy.11 = bf16[1,32,2048]{2,1,0:T(8,128)(2,1)} copy(bf16[1,32,2048]{2,1,0:T(8,128)(2,1)} %bitcast.10) | data formatting | bytes 262144

commit v3 on v2

--- a/solution.py
+++ b/solution.py
@@ -10,7 +10,6 @@
 HEAD_DIM = 128
 EPSILON = 1e-05
 FLOOR = -1e30
-TILE = 512
 MESH = pl.DeviceIdType.MESH
 F32 = jnp.float32
 BF16 = jnp.bfloat16
@@ -69,9 +68,9 @@
     group = (heads_per * n_col) // kv_heads
     tall = group * samples
     mine = kv_heads // n_row
-    q_tiles = qw_ref.shape[1] // TILE
-    tiles = units * HEAD_DIM // TILE
-    pair_cols = kvw_ref.shape[1]
+    tile = quarter * HEAD_DIM
+    half = width // 2
+    is_end = jnp.logical_or(col == 0, col == n_col - 1)
 
     mate = row + 1 - 2 * (row % 2)
     across = (row + 2) % 4
@@ -80,31 +79,24 @@
     def peer(d):
         return lax.rem(row + d, n_row)
 
-    loads = []
-    for t in range(q_tiles):
-        loads.append(
-            pltpu.make_async_copy(
-                qw_ref.at[:, pl.ds(t * TILE, TILE)], weights.at[t], weight_sem.at[t]
-            )
-        )
-    for t in range(q_tiles, tiles):
-        first = (t - q_tiles) * TILE
-        wide = min(TILE, pair_cols - first)
-        if wide > 0:
+    cache_load = pltpu.make_async_copy(cache_ref, cache, cache_sem)
+    cache_load.start()
+    loads, filled = [], 0
+    for source in (qw_ref, kvw_ref):
+        taken = 0
+        while taken < source.shape[1]:
+            t, at = filled // tile, filled % tile
+            wide = min(source.shape[1] - taken, tile - at)
             loads.append(
                 pltpu.make_async_copy(
-                    kvw_ref.at[:, pl.ds(first, wide)],
-                    weights.at[t, :, pl.ds(0, wide)],
-                    weight_sem.at[t],
+                    source.at[:, pl.ds(taken, wide)],
+                    weights.at[t, :, pl.ds(at, wide)],
+                    weight_sem.at[len(loads)],
                 )
             )
-        else:
-            loads.append(None)
-    cache_load = pltpu.make_async_copy(cache_ref, cache, cache_sem)
-    cache_load.start()
+            taken, filled = taken + wide, filled + wide
     for load in loads:
-        if load is not None:
-            load.start()
+        load.start()
 
     barrier = pltpu.get_barrier_semaphore()
     for d in range(1, n_row):
@@ -117,38 +109,41 @@
         barrier, inc=1, device_id=(lax.rem(sec + n_sec - 1, n_sec), row, col), device_id_type=MESH
     )
 
-    for t in range(q_tiles, tiles):
-        first = (t - q_tiles) * TILE
-        wide = max(0, min(TILE, pair_cols - first))
-        if wide < TILE:
-            weights[t, :, wide:] = jnp.zeros((width, TILE - wide), BF16)
+    while filled < n_row * tile:
+        t, at = filled // tile, filled % tile
+        weights[t, :, at:] = jnp.zeros((width, tile - at), BF16)
+        filled = (t + 1) * tile
     widened = hidden_ref[...].astype(F32)
-    gathered[col] = (widened * gain_ref[...]).astype(BF16)
+    for h in range(2):
+        some = slice(h * half, (h + 1) * half)
+        gathered[col, h] = (widened[:, some] * gain_ref[:, some]).astype(BF16)
     squares[row] = jnp.broadcast_to(
         jnp.sum(widened * widened, axis=1, keepdims=True), (rows, HEAD_DIM)
     )
 
     pl.semaphore_wait(barrier, n_row - 1 + n_col - 1 + 1)
 
-    def gather_copy(block, to, send_sem):
-        return pltpu.make_async_remote_copy(
-            src_ref=gathered.at[block],
-            dst_ref=gathered.at[block],
-            send_sem=send_sem,
-            recv_sem=gather_recv.at[block],
+    def gather_copy(block, h, to, send_sem):
+        return pltpu.make_async_remote_copy(
+            src_ref=gathered.at[block, h],
+            dst_ref=gathered.at[block, h],
+            send_sem=send_sem.at[h],
+            recv_sem=gather_recv.at[block, h],
             device_id=(sec, row, to),
             device_id_type=MESH,
         )
 
     below, above = jnp.maximum(col - 1, 0), jnp.minimum(col + 1, n_col - 1)
 
-    @pl.when(col > 0)
-    def _():
-        gather_copy(col, below, gather_send.at[col]).start()
-
-    @pl.when(col < n_col - 1)
-    def _():
-        gather_copy(col, above, own_send).start()
+    for h in range(2):
+
+        @pl.when(col > 0)
+        def _():
+            gather_copy(col, h, below, gather_send.at[col]).start()
+
+        @pl.when(col < n_col - 1)
+        def _():
+            gather_copy(col, h, above, own_send).start()
 
     def square_copy(d):
         return pltpu.make_async_remote_copy(
@@ -187,17 +182,35 @@
     upward = col < n_col - 1 - col
 
     def block_at(k):
-        half = (k + 1) // 2
-        near = jnp.where(k % 2 == 1, col + half, col - half)
+        away = (k + 1) // 2
+        near = jnp.where(k % 2 == 1, col + away, col - away)
         far = jnp.where(upward, col + (k - shorter), col - (k - shorter))
         return jnp.where(k <= 2 * shorter, near, far)
 
-    def sum_copy(block, d):
-        other = peer(d)
+    def pass_on(k, h):
+        block = block_at(k)
+        gather_copy(block, h, below, gather_send.at[block]).wait_recv()
+
+        @pl.when(block > col)
+        def _():
+            gather_copy(block, h, below, gather_send.at[block]).start()
+
+        @pl.when(block < col)
+        def _():
+            gather_copy(block, h, above, gather_send.at[block]).start()
+
+    @pl.when(jnp.logical_not(is_end))
+    def _():
+        for first in range(1, n_col, 2):
+            for h in range(2):
+                for k in range(first, min(first + 2, n_col)):
+                    pass_on(k, h)
+
+    def sum_copy(block, other):
         return pltpu.make_async_remote_copy(
             src_ref=parts.at[block, pl.ds(other * quarter, quarter)],
             dst_ref=arrived.at[block, row],
-            send_sem=sum_send.at[block, d],
+            send_sem=sum_send.at[block, other],
             recv_sem=sum_recv.at[block, row],
             device_id=(sec, other, col),
             device_id_type=MESH,
@@ -262,45 +275,63 @@
             summed[block] = total
             turn_copy(block).start()
 
-    def step(k, carry):
-        block = block_at(k)
-
-        @pl.when(k > 0)
-        def _():
-            gather_copy(block, below, gather_send.at[block]).wait_recv()
-
-        @pl.when(jnp.logical_and(block > col, col > 0))
-        def _():
-            gather_copy(block, below, gather_send.at[block]).start()
-
-        @pl.when(jnp.logical_and(block < col, col < n_col - 1))
-        def _():
-            gather_copy(block, above, gather_send.at[block]).start()
-
-        for t in range(tiles):
-            if loads[t] is not None:
-
-                @pl.when(k == 0)
+    for load in loads:
+        load.wait()
+
+    step_blocks = 2
+
+    def target(j):
+        return jnp.where(
+            j == 0, across, jnp.where(j == 1, far_peer, jnp.where(j == 2, mate, row))
+        )
+
+    def step(s, carry):
+        blocks = [block_at(step_blocks * s + i) for i in range(step_blocks)]
+
+        @pl.when(is_end)
+        def _():
+            for i, block in enumerate(blocks):
+
+                @pl.when(step_blocks * s + i > 0)
                 def _():
-                    loads[t].wait()
-
-            product = jnp.dot(gathered[block], weights[t], preferred_element_type=F32)
+                    for h in range(2):
+                        gather_copy(block, h, below, gather_send.at[block]).wait_recv()
+
+        def multiply(j, carry):
+            dest = target(j)
+            product = jnp.zeros((step_blocks * rows, tile), F32)
+            for h in range(2):
+                taken = jnp.concatenate([gathered[block, h] for block in blocks], axis=0)
+                product = product + jnp.dot(
+                    taken, weights[dest, h * half : (h + 1) * half], preferred_element_type=F32
+                )
             product = product.astype(BF16)
-            for u in range(TILE // HEAD_DIM):
-                parts[block, t * (TILE // HEAD_DIM) + u] = product[
-                    :, u * HEAD_DIM : (u + 1) * HEAD_DIM
-                ]
-        for d in range(1, n_row):
-            sum_copy(block, d).start()
-
-        @pl.when(k > 0)
-        def _():
-            reduce_block(block_at(k - 1))
-
+            for i, block in enumerate(blocks):
+                for u in range(quarter):
+                    parts[block, dest * quarter + u] = product[
+                        i * rows : (i + 1) * rows, u * HEAD_DIM : (u + 1) * HEAD_DIM
+                    ]
+
+            @pl.when(j < n_row - 1)
+            def _():
+                for block in blocks:
+                    sum_copy(block, dest).start()
+
+            return carry
+
+        lax.fori_loop(0, n_row // 2, multiply, 0)
+
+        @pl.when(s > 0)
+        def _():
+            for i in range(step_blocks):
+                reduce_block(block_at(step_blocks * (s - 1) + i))
+
+        lax.fori_loop(n_row // 2, n_row, multiply, 0)
         return carry
 
-    lax.fori_loop(0, n_col, step, 0)
-    reduce_block(block_at(n_col - 1))
+    lax.fori_loop(0, n_col // step_blocks, step, 0)
+    for i in range(step_blocks):
+        reduce_block(block_at(n_col - step_blocks + i))
 
     def forward(k, carry):
         source = block_at(k)
@@ -385,11 +416,11 @@
         for (g, p), product in zip(pairs, products):
             outs[g, p] = product.astype(BF16)
         for i, g in enumerate(heads):
-            tile = jnp.zeros((tall, HEAD_DIM), F32)
+            both = jnp.zeros((tall, HEAD_DIM), F32)
             for p in range(prompts):
-                tile = jnp.where(lane == 2 * p, tops[i * prompts + p], tile)
-                tile = jnp.where(lane == 2 * p + 1, totals[i * prompts + p], tile)
-            stat_rows[g] = tile.T[:8]
+                both = jnp.where(lane == 2 * p, tops[i * prompts + p], both)
+                both = jnp.where(lane == 2 * p + 1, totals[i * prompts + p], both)
+            stat_rows[g] = both.T[:8]
 
     def out_copy(dest):
         return pltpu.make_async_remote_copy(
@@ -419,7 +450,7 @@
     def chunk(k, carry):
         j = k
         if by_dest:
-            j = jnp.where(k == 0, across, jnp.where(k == 1, far_peer, jnp.where(k == 2, mate, row)))
+            j = target(k)
         for i in range(chunk_cols):
             source = j * chunk_cols + i
             full_copy(source, mate, mate, 1).wait_recv()
@@ -512,32 +543,30 @@
                 ]
         hand_copy(i).start()
 
-    @pl.when(col > 0)
-    def _():
-        gather_copy(col, below, gather_send.at[col]).wait_send()
-
-    @pl.when(col < n_col - 1)
-    def _():
-        gather_copy(col, above, own_send).wait_send()
+    for h in range(2):
+
+        @pl.when(col > 0)
+        def _():
+            gather_copy(col, h, below, gather_send.at[col]).wait_send()
+
+        @pl.when(col < n_col - 1)
+        def _():
+            gather_copy(col, h, above, own_send).wait_send()
 
     def drain(k, carry):
         block = block_at(k)
 
-        @pl.when(
-            jnp.logical_or(
-                jnp.logical_and(block > col, col > 0),
-                jnp.logical_and(block < col, col < n_col - 1),
-            )
-        )
-        def _():
-            gather_copy(block, below, gather_send.at[block]).wait_send()
+        @pl.when(jnp.logical_and(block != col, jnp.logical_not(is_end)))
+        def _():
+            for h in range(2):
+                gather_copy(block, h, below, gather_send.at[block]).wait_send()
 
         @pl.when(block != col)
         def _():
             turn_copy(block).wait_send()
 
         for d in range(1, n_row):
-            sum_copy(block, d).wait_send()
+            sum_copy(block, peer(d)).wait_send()
         full_copy(block, row, across, 0).wait_send()
         full_copy(block, row, mate, 1).wait_send()
         full_copy(block, across, mate, 2).wait_send()
@@ -563,7 +592,6 @@
     group = heads_per * n_col // kv_heads
     tall = group * (rows // prompts)
     mine = kv_heads // n_row
-    tiles = units * HEAD_DIM // TILE
     dims = (n_sec, n_row, n_col, units, quarter, heads_per, pairs_per, kv_heads)
     dma = pltpu.SemaphoreType.DMA
     vmem = pl.BlockSpec(memory_space=pltpu.VMEM)
@@ -584,11 +612,11 @@
         ],
         out_specs=(vmem, vmem),
         scratch_shapes=[
-            pltpu.VMEM((tiles, width, TILE), BF16),
+            pltpu.VMEM((n_row, width, quarter * HEAD_DIM), BF16),
             pltpu.VMEM((prompts, positions, 2, cache_width), BF16),
             pltpu.VMEM((prompts, positions, cache_width), BF16),
             pltpu.VMEM((prompts, positions, cache_width), BF16),
-            pltpu.VMEM((n_col, rows, width), BF16),
+            pltpu.VMEM((n_col, 2, rows, width // 2), BF16),
             pltpu.VMEM((n_col, units, rows, HEAD_DIM), BF16),
             pltpu.VMEM((n_col, n_row, quarter, rows, HEAD_DIM), BF16),
             pltpu.VMEM((n_col, quarter, rows, HEAD_DIM), BF16),
@@ -599,11 +627,11 @@
             pltpu.VMEM((n_row, mine, 8, tall), F32),
             pltpu.VMEM((n_row, rows, HEAD_DIM), F32),
             pltpu.VMEM((rows, heads_per * n_col // n_row * HEAD_DIM), BF16),
-            dma((tiles,)),
+            dma((2 * n_row + 2,)),
             dma,
-            dma((n_col,)),
-            dma((n_col,)),
-            dma,
+            dma((n_col, 2)),
+            dma((n_col, 2)),
+            dma((2,)),
             dma((n_col, n_row)),
             dma((n_col, n_row)),
             dma((n_col,)),
@@ -620,7 +648,7 @@
             dma((mine,)),
         ],
         compiler_params=pltpu.CompilerParams(
-            collective_id=0, has_side_effects=True, vmem_limit_bytes=60 * 1024 * 1024
+            collective_id=0, has_side_effects=True, vmem_limit_bytes=52 * 1024 * 1024
         ),
     )(
         hidden_in[0],

time: 56.6 us -> 51.8 us (0.915)
  the two profiles are of different devices: /device:TPU:2 before, /device:TPU:10 now
where the time goes in v3:
time: 51.8 us; the launch traced here: 51.6 us
  Pallas kernels  47.3 us (91%)
  local copies, waits for them, and re-layouts  3.56 us (7%)
  between operations  0.65 us (1%)
    pallas_call x1, Pallas kernels, shards(): pl.pallas_call(functools.partial(kernel, dims), out_shape=(jax.ShapeDtype...  47.3 us
    unnamed x8, local copies, waits for them, and re-layouts  3.56 us

profile of v3, /device:TPU:10, one launch (start us, length us, event | category | flops | bytes accessed | tf_op | source)
XLA Modules:
  0.0 51.6 jit_solution(17596610451307151414)
XLA Ops:
  0.6 0.0 copy-start
  0.6 0.9 %copy-done = bf16[1,32,2048]{2,1,0:T(8,128)(2,1)S(1)} copy-done((bf16[1,32,2048]{2,1,0:T(8,128)(2,1)S(1)}, bf16[1,32,2048]{2,1,0:T(8,128)(2,1)}, u32[]{:S(2)}) %copy-start) | copy-done | bytes 131096
  1.5 0.0 copy-start.1
  1.5 0.7 %copy-done.1 = f32[1,2048]{1,0:T(1,128)S(1)} copy-done((f32[1,2048]{1,0:T(1,128)S(1)}, f32[1,2048]{1,0:T(1,128)}, u32[]{:S(2)}) %copy-start.1) | copy-done | bytes 8216
  2.2 0.0 copy-start.2
  2.2 0.7 %copy-done.2 = s32[1,2]{1,0:T(1,128)S(1)} copy-done((s32[1,2]{1,0:T(1,128)S(1)}, s32[1,2]{1,0:T(1,128)}, u32[]{:S(2)}) %copy-start.2) | copy-done | bytes 32
  2.9 47.3 %shard_map.77 = (bf16[32,2048]{1,0:T(8,128)(2,1)S(1)}, bf16[32,2048]{1,0:T(8,128)(2,1)S(1)}) custom-call(bf16[32,2048]{1,0:T(8,128)(2,1)S(1)} %bitcast.6, f32[1,2048]{1,0:T(1,128)S(1)} %copy-done.1, bf16[2048,2048]{1,0:T(8,128)(2,1)} %bitcast.9, bf16[2048,512]{1,0:T(8,128)(2,1)} %bitcast.10, bf16[2,256,2,1024]{3,2,1,0:T(2,128)(2,1)} %bitcast.11, ...), custom_call_target="tpu_custom_call" | custom-call | tf_op jit(solution)/shard_map/pallas_call | solution.py:599
  50.2 0.7 %copy.10 = bf16[1,32,2048]{2,1,0:T(8,128)(2,1)} copy(bf16[1,32,2048]{2,1,0:T(8,128)(2,1)S(1)} %bitcast.8) | data formatting | bytes 262144
  50.9 0.7 %copy.11 = bf16[1,32,2048]{2,1,0:T(8,128)(2,1)} copy(bf16[1,32,2048]{2,1,0:T(8,128)(2,1)S(1)} %bitcast.7) | data formatting | bytes 262144
Async XLA Ops:
  0.6 0.9 %copy-start = (bf16[1,32,2048]{2,1,0:T(8,128)(2,1)S(1)}, bf16[1,32,2048]{2,1,0:T(8,128)(2,1)}, u32[]{:S(2)}) copy-start(bf16[1,32,2048]{2,1,0:T(8,128)(2,1)} %param.6) | copy-start | bytes 393220
  1.5 0.7 %copy-start.1 = (f32[1,2048]{1,0:T(1,128)S(1)}, f32[1,2048]{1,0:T(1,128)}, u32[]{:S(2)}) copy-start(f32[1,2048]{1,0:T(1,128)} %gain_ref.1) | copy-start | bytes 24580
  2.2 0.7 %copy-start.2 = (s32[1,2]{1,0:T(1,128)S(1)}, s32[1,2]{1,0:T(1,128)}, u32[]{:S(2)}) copy-start(s32[1,2]{1,0:T(1,128)} %len_ref.1) | copy-start | bytes 28

commit v4 on v3

--- a/solution.py
+++ b/solution.py
@@ -18,17 +18,21 @@
 def kernel(
     dims,
     hidden_ref,
-    gain_ref,
+    gain_hbm,
     qw_ref,
     kvw_ref,
     cache_ref,
-    len_ref,
+    len_hbm,
     handed_ref,
+    newkv_hbm,
     newkv_ref,
     weights,
     cache,
     keys,
     values,
+    gain_ref,
+    len_ref,
+    scaled_rows,
     gathered,
     parts,
     arrived,
@@ -42,6 +46,7 @@
     final,
     weight_sem,
     cache_sem,
+    small_sem,
     gather_send,
     gather_recv,
     own_send,
@@ -79,8 +84,17 @@
     def peer(d):
         return lax.rem(row + d, n_row)
 
+    own_loads = [
+        pltpu.make_async_copy(
+            hidden_ref.at[:, pl.ds(h * half, half)], gathered.at[col, h], small_sem.at[h]
+        )
+        for h in range(2)
+    ]
+    gain_load = pltpu.make_async_copy(gain_hbm, gain_ref, small_sem.at[2])
+    len_load = pltpu.make_async_copy(len_hbm, len_ref, small_sem.at[3])
     cache_load = pltpu.make_async_copy(cache_ref, cache, cache_sem)
-    cache_load.start()
+    for load in own_loads + [gain_load, len_load, cache_load]:
+        load.start()
     loads, filled = [], 0
     for source in (qw_ref, kvw_ref):
         taken = 0
@@ -113,14 +127,6 @@
         t, at = filled // tile, filled % tile
         weights[t, :, at:] = jnp.zeros((width, tile - at), BF16)
         filled = (t + 1) * tile
-    widened = hidden_ref[...].astype(F32)
-    for h in range(2):
-        some = slice(h * half, (h + 1) * half)
-        gathered[col, h] = (widened[:, some] * gain_ref[:, some]).astype(BF16)
-    squares[row] = jnp.broadcast_to(
-        jnp.sum(widened * widened, axis=1, keepdims=True), (rows, HEAD_DIM)
-    )
-
     pl.semaphore_wait(barrier, n_row - 1 + n_col - 1 + 1)
 
     def gather_copy(block, h, to, send_sem):
@@ -133,17 +139,35 @@
             device_id_type=MESH,
         )
 
+    def own_copy(h, to, send_sem):
+        return pltpu.make_async_remote_copy(
+            src_ref=hidden_ref.at[:, pl.ds(h * half, half)],
+            dst_ref=gathered.at[col, h],
+            send_sem=send_sem.at[h],
+            recv_sem=gather_recv.at[col, h],
+            device_id=(sec, row, to),
+            device_id_type=MESH,
+        )
+
     below, above = jnp.maximum(col - 1, 0), jnp.minimum(col + 1, n_col - 1)
 
     for h in range(2):
 
         @pl.when(col > 0)
         def _():
-            gather_copy(col, h, below, gather_send.at[col]).start()
+            own_copy(h, below, gather_send.at[col]).start()
 
         @pl.when(col < n_col - 1)
         def _():
-            gather_copy(col, h, above, own_send).start()
+            own_copy(h, above, own_send).start()
+
+    for load in own_loads:
+        load.wait()
+    square = jnp.zeros((rows, 1), F32)
+    for h in range(2):
+        widened = gathered[col, h].astype(F32)
+        square = square + jnp.sum(widened * widened, axis=1, keepdims=True)
+    squares[row] = jnp.broadcast_to(square, (rows, HEAD_DIM))
 
     def square_copy(d):
         return pltpu.make_async_remote_copy(
@@ -176,8 +200,6 @@
         values[p, :, some] = apart[positions:]
         return carry
 
-    lax.fori_loop(0, prompts * strips, split, 0)
-
     shorter = jnp.minimum(col, n_col - 1 - col)
     upward = col < n_col - 1 - col
 
@@ -199,12 +221,21 @@
         def _():
             gather_copy(block, h, above, gather_send.at[block]).start()
 
-    @pl.when(jnp.logical_not(is_end))
-    def _():
-        for first in range(1, n_col, 2):
-            for h in range(2):
-                for k in range(first, min(first + 2, n_col)):
-                    pass_on(k, h)
+    in_middle = jnp.logical_not(is_end)
+    ways = prompts * strips
+    for h in range(2):
+        lax.fori_loop(h * ways // 2, (h + 1) * ways // 2, split, 0)
+
+        @pl.when(in_middle)
+        def _():
+            for k in range(1, min(3, n_col)):
+                pass_on(k, h)
+
+    def pass_late(h):
+        @pl.when(in_middle)
+        def _():
+            for k in range(3, n_col):
+                pass_on(k, h)
 
     def sum_copy(block, other):
         return pltpu.make_async_remote_copy(
@@ -278,32 +309,41 @@
     for load in loads:
         load.wait()
 
-    step_blocks = 2
+    gain_load.wait()
 
     def target(j):
         return jnp.where(
             j == 0, across, jnp.where(j == 1, far_peer, jnp.where(j == 2, mate, row))
         )
 
-    def step(s, carry):
-        blocks = [block_at(step_blocks * s + i) for i in range(step_blocks)]
+    def step(first, count, before, between):
+        blocks = [block_at(first + i) for i in range(count)]
 
         @pl.when(is_end)
         def _():
             for i, block in enumerate(blocks):
 
-                @pl.when(step_blocks * s + i > 0)
+                @pl.when(first + i > 0)
                 def _():
                     for h in range(2):
                         gather_copy(block, h, below, gather_send.at[block]).wait_recv()
 
+        before()
+        for i, block in enumerate(blocks):
+            for h in range(2):
+                raw = gathered[block, h].astype(F32)
+                scaled_rows[h, i * rows : (i + 1) * rows] = (
+                    raw * gain_ref[:, h * half : (h + 1) * half]
+                ).astype(BF16)
+
         def multiply(j, carry):
             dest = target(j)
-            product = jnp.zeros((step_blocks * rows, tile), F32)
+            product = jnp.zeros((count * rows, tile), F32)
             for h in range(2):
-                taken = jnp.concatenate([gathered[block, h] for block in blocks], axis=0)
                 product = product + jnp.dot(
-                    taken, weights[dest, h * half : (h + 1) * half], preferred_element_type=F32
+                    scaled_rows[h, : count * rows],
+                    weights[dest, h * half : (h + 1) * half],
+                    preferred_element_type=F32,
                 )
             product = product.astype(BF16)
             for i, block in enumerate(blocks):
@@ -320,18 +360,24 @@
             return carry
 
         lax.fori_loop(0, n_row // 2, multiply, 0)
-
-        @pl.when(s > 0)
-        def _():
-            for i in range(step_blocks):
-                reduce_block(block_at(step_blocks * (s - 1) + i))
-
+        between()
         lax.fori_loop(n_row // 2, n_row, multiply, 0)
+
+    step(0, 2, lambda: pass_late(0), lambda: pass_late(1))
+
+    def single(k, carry):
+        def between():
+            @pl.when(k == 2)
+            def _():
+                reduce_block(block_at(0))
+
+            reduce_block(block_at(k - 1))
+
+        step(k, 1, lambda: None, between)
         return carry
 
-    lax.fori_loop(0, n_col // step_blocks, step, 0)
-    for i in range(step_blocks):
-        reduce_block(block_at(n_col - step_blocks + i))
+    lax.fori_loop(2, n_col, single, 0)
+    reduce_block(block_at(n_col - 1))
 
     def forward(k, carry):
         source = block_at(k)
@@ -363,6 +409,7 @@
     square_sum = squares[0]
     for i in range(1, n_row):
         square_sum = square_sum + squares[i]
+    len_load.wait()
     scaling = lax.rsqrt(square_sum / (width * n_row) + EPSILON)
 
     def head_unit(head):
@@ -476,6 +523,9 @@
             full[pair_unit(pair)].astype(F32) * scaling
         ).astype(BF16)
 
+    newkv_store = pltpu.make_async_copy(newkv_ref, newkv_hbm, small_sem.at[4])
+    newkv_store.start()
+
     def own_part(g, p):
         new_key = jnp.concatenate([scaled(pair_unit(g), p)] * group, axis=0)
         product = queries(g, p).astype(F32) * new_key.astype(F32)
@@ -547,11 +597,11 @@
 
         @pl.when(col > 0)
         def _():
-            gather_copy(col, h, below, gather_send.at[col]).wait_send()
+            own_copy(h, below, gather_send.at[col]).wait_send()
 
         @pl.when(col < n_col - 1)
         def _():
-            gather_copy(col, h, above, own_send).wait_send()
+            own_copy(h, above, own_send).wait_send()
 
     def drain(k, carry):
         block = block_at(k)
@@ -577,8 +627,20 @@
         square_copy(d).wait_send()
         stat_copy(peer(d)).wait_send()
         out_copy(peer(d)).wait_send()
+    newkv_store.wait()
     for i in range(mine):
         hand_copy(i).wait()
+
+
+def copy_both(first_ref, second_ref, first_out, second_out, sem):
+    copies = [
+        pltpu.make_async_copy(first_ref, first_out, sem.at[0]),
+        pltpu.make_async_copy(second_ref, second_out, sem.at[1]),
+    ]
+    for copy in copies:
+        copy.start()
+    for copy in copies:
+        copy.wait()
 
 
 def shards(n_sec, n_row, n_col, hidden_in, norm_gain, q_weight, kv_weight, kv_cache, lengths):
@@ -594,28 +656,23 @@
     mine = kv_heads // n_row
     dims = (n_sec, n_row, n_col, units, quarter, heads_per, pairs_per, kv_heads)
     dma = pltpu.SemaphoreType.DMA
-    vmem = pl.BlockSpec(memory_space=pltpu.VMEM)
-    anywhere = pl.BlockSpec(memory_space=pl.ANY)
     handed, new_kv = pl.pallas_call(
         functools.partial(kernel, dims),
         out_shape=(
             jax.ShapeDtypeStruct((rows, heads_per * n_col // n_row * HEAD_DIM), BF16),
             jax.ShapeDtypeStruct((rows, 2 * cache_width), BF16),
         ),
-        in_specs=[
-            vmem,
-            vmem,
-            anywhere,
-            anywhere,
-            anywhere,
-            pl.BlockSpec(memory_space=pltpu.SMEM),
-        ],
-        out_specs=(vmem, vmem),
+        in_specs=[pl.BlockSpec(memory_space=pltpu.HBM)] * 6,
+        out_specs=[pl.BlockSpec(memory_space=pltpu.HBM)] * 2,
         scratch_shapes=[
+            pltpu.VMEM((rows, 2 * cache_width), BF16),
             pltpu.VMEM((n_row, width, quarter * HEAD_DIM), BF16),
             pltpu.VMEM((prompts, positions, 2, cache_width), BF16),
             pltpu.VMEM((prompts, positions, cache_width), BF16),
             pltpu.VMEM((prompts, positions, cache_width), BF16),
+            pltpu.VMEM((1, width), F32),
+            pltpu.SMEM((1, prompts), jnp.int32),
+            pltpu.VMEM((2, 2 * rows, width // 2), BF16),
             pltpu.VMEM((n_col, 2, rows, width // 2), BF16),
             pltpu.VMEM((n_col, units, rows, HEAD_DIM), BF16),
             pltpu.VMEM((n_col, n_row, quarter, rows, HEAD_DIM), BF16),
@@ -629,6 +686,7 @@
             pltpu.VMEM((rows, heads_per * n_col // n_row * HEAD_DIM), BF16),
             dma((2 * n_row + 2,)),
             dma,
+            dma((5,)),
             dma((n_col, 2)),
             dma((n_col, 2)),
             dma((2,)),
@@ -648,7 +706,7 @@
             dma((mine,)),
         ],
         compiler_params=pltpu.CompilerParams(
-            collective_id=0, has_side_effects=True, vmem_limit_bytes=52 * 1024 * 1024
+            collective_id=0, has_side_effects=True, vmem_limit_bytes=60 * 1024 * 1024
         ),
     )(
         hidden_in[0],
@@ -658,6 +716,14 @@
         kv_cache[0],
         lengths,
     )
+    outputs = (handed, new_kv)
+    handed, new_kv = pl.pallas_call(
+        copy_both,
+        out_shape=tuple(jax.ShapeDtypeStruct(x.shape, x.dtype) for x in outputs),
+        in_specs=[pl.BlockSpec(memory_space=pl.ANY)] * 2,
+        out_specs=[pl.BlockSpec(memory_space=pltpu.HBM)] * 2,
+        scratch_shapes=[dma((2,))],
+    )(*outputs)
     return handed[None], new_kv[None]
 
 

time: 51.8 us -> 54.8 us (1.058)
  the two profiles are of different devices: /device:TPU:10 before, /device:TPU:2 now
where the time goes in v4:
time: 54.8 us; the launch traced here: 54.6 us
  Pallas kernels  54 us (99%)
  between operations  0.64 us (1%)
    pallas_call x1, Pallas kernels, shards(): pl.pallas_call(functools.partial(kernel, dims), out_shape=(jax.ShapeDtype...  44.9 us
    pallas_call x1, Pallas kernels, shards(): pl.pallas_call(copy_both, out_shape=tuple((jax.ShapeDtypeStruct(x.shape,...  9.06 us

profile of v4, /device:TPU:2, one launch (start us, length us, event | category | flops | bytes accessed | tf_op | source)
XLA Modules:
  0.0 54.6 jit_solution(501402390764754168)
XLA Ops:
  0.6 44.9 %shard_map.77 = (bf16[32,2048]{1,0:T(8,128)(2,1)}, bf16[32,2048]{1,0:T(8,128)(2,1)}) custom-call(bf16[32,2048]{1,0:T(8,128)(2,1)} %bitcast.9, f32[1,2048]{1,0:T(1,128)} %gain_hbm.1, bf16[2048,2048]{1,0:T(8,128)(2,1)} %bitcast.6, bf16[2048,512]{1,0:T(8,128)(2,1)} %bitcast.7, bf16[2,256,2,1024]{3,2,1,0:T(2,128)(2,1)} %bitcast.8, s32[1,2]{1,0:T(1,128)} %len_hbm.1), custom_call_target="tpu_custom_call" | custom-call | tf_op jit(solution)/shard_map/pallas_call | solution.py:659
  45.6 9.1 %shard_map.78 = (bf16[32,2048]{1,0:T(8,128)(2,1)}, bf16[32,2048]{1,0:T(8,128)(2,1)}) custom-call(bf16[32,2048]{1,0:T(8,128)(2,1)} %get-tuple-element.6.first_ref, bf16[32,2048]{1,0:T(8,128)(2,1)} %get-tuple-element.7.second_ref), custom_call_target="tpu_custom_call" | custom-call | tf_op jit(solution)/shard_map/pallas_call | solution.py:720

commit v5 on v4

--- a/solution.py
+++ b/solution.py
@@ -24,7 +24,6 @@
     cache_ref,
     len_hbm,
     handed_ref,
-    newkv_hbm,
     newkv_ref,
     weights,
     cache,
@@ -379,22 +378,7 @@
     lax.fori_loop(2, n_col, single, 0)
     reduce_block(block_at(n_col - 1))
 
-    def forward(k, carry):
-        source = block_at(k)
-        pltpu.make_async_remote_copy(
-            src_ref=full_part(source, row),
-            dst_ref=full_part(source, row),
-            send_sem=turn_send.at[source],
-            recv_sem=turn_recv.at[source],
-            device_id=(sec, row, source),
-            device_id_type=MESH,
-        ).wait_recv()
-        spread(source)
-        relay(block_at(k - 1))
-        return carry
-
-    lax.fori_loop(1, n_col, forward, 0)
-    relay(block_at(n_col - 1))
+    relay(col)
 
     for d in range(1, n_row):
         other = peer(d)
@@ -482,7 +466,10 @@
     chunk_heads = max(1, heads_per // group)
     chunk_cols = max(1, group // heads_per)
     chunks = kv_heads // chunk_heads
-    by_dest = chunks == n_row and chunk_heads == mine
+    by_dest = chunks == n_row and chunk_heads == mine and chunks == n_col
+    col_turn = jnp.where(
+        col == across, 0, jnp.where(col == far_peer, 1, jnp.where(col == mate, 2, 3))
+    )
 
     def stat_copy(dest):
         return pltpu.make_async_remote_copy(
@@ -497,7 +484,7 @@
     def chunk(k, carry):
         j = k
         if by_dest:
-            j = target(k)
+            j = jnp.where(k == 0, col, target(jnp.where(k > col_turn, k, k - 1)))
         for i in range(chunk_cols):
             source = j * chunk_cols + i
             full_copy(source, mate, mate, 1).wait_recv()
@@ -513,7 +500,33 @@
 
         return carry
 
-    lax.fori_loop(0, chunks, chunk, 0)
+    early = 1 if by_dest else 0
+    lax.fori_loop(0, early, chunk, 0)
+
+    def forward(k, carry):
+        source = block_at(k)
+        pltpu.make_async_remote_copy(
+            src_ref=full_part(source, row),
+            dst_ref=full_part(source, row),
+            send_sem=turn_send.at[source],
+            recv_sem=turn_recv.at[source],
+            device_id=(sec, row, source),
+            device_id_type=MESH,
+        ).wait_recv()
+        spread(source)
+
+        @pl.when(k > 1)
+        def _():
+            relay(block_at(k - 1))
+
+        return carry
+
+    lax.fori_loop(1, n_col, forward, 0)
+
+    @pl.when(n_col > 1)
+    def _():
+        relay(block_at(n_col - 1))
+    lax.fori_loop(early, chunks, chunk, 0)
 
     outs_in[row] = outs[pl.ds(row * mine, mine)]
     stat_in[row] = stat_rows[pl.ds(row * mine, mine)]
@@ -522,9 +535,6 @@
         newkv_ref[:, pair * HEAD_DIM : (pair + 1) * HEAD_DIM] = (
             full[pair_unit(pair)].astype(F32) * scaling
         ).astype(BF16)
-
-    newkv_store = pltpu.make_async_copy(newkv_ref, newkv_hbm, small_sem.at[4])
-    newkv_store.start()
 
     def own_part(g, p):
         new_key = jnp.concatenate([scaled(pair_unit(g), p)] * group, axis=0)
@@ -556,12 +566,13 @@
     stats = jnp.concatenate([lines, jnp.zeros((HEAD_DIM - n_row * mine * 8, tall), F32)], axis=0).T
     span = group * HEAD_DIM
 
-    def hand_copy(i):
-        return pltpu.make_async_remote_copy(
-            src_ref=final.at[:, pl.ds(i * span, span)],
-            dst_ref=handed_ref.at[:, pl.ds(i * span, span)],
-            send_sem=hand_send.at[i],
-            recv_sem=hand_recv.at[i],
+    def hand_copy(i, p):
+        piece = (pl.ds(p * samples, samples), pl.ds(i * span, span))
+        return pltpu.make_async_remote_copy(
+            src_ref=final.at[piece],
+            dst_ref=handed_ref.at[piece],
+            send_sem=hand_send.at[i, p],
+            recv_sem=hand_recv.at[i, p],
             device_id=(lax.rem(sec + 1, n_sec), row, col),
             device_id_type=MESH,
         )
@@ -591,7 +602,7 @@
                 final[p * samples : (p + 1) * samples, first : first + HEAD_DIM] = done[
                     h * samples : (h + 1) * samples
                 ]
-        hand_copy(i).start()
+            hand_copy(i, p).start()
 
     for h in range(2):
 
@@ -627,20 +638,9 @@
         square_copy(d).wait_send()
         stat_copy(peer(d)).wait_send()
         out_copy(peer(d)).wait_send()
-    newkv_store.wait()
     for i in range(mine):
-        hand_copy(i).wait()
-
-
-def copy_both(first_ref, second_ref, first_out, second_out, sem):
-    copies = [
-        pltpu.make_async_copy(first_ref, first_out, sem.at[0]),
-        pltpu.make_async_copy(second_ref, second_out, sem.at[1]),
-    ]
-    for copy in copies:
-        copy.start()
-    for copy in copies:
-        copy.wait()
+        for p in range(prompts):
+            hand_copy(i, p).wait()
 
 
 def shards(n_sec, n_row, n_col, hidden_in, norm_gain, q_weight, kv_weight, kv_cache, lengths):
@@ -663,9 +663,8 @@
             jax.ShapeDtypeStruct((rows, 2 * cache_width), BF16),
         ),
         in_specs=[pl.BlockSpec(memory_space=pltpu.HBM)] * 6,
-        out_specs=[pl.BlockSpec(memory_space=pltpu.HBM)] * 2,
+        out_specs=[pl.BlockSpec(memory_space=pltpu.VMEM)] * 2,
         scratch_shapes=[
-            pltpu.VMEM((rows, 2 * cache_width), BF16),
             pltpu.VMEM((n_row, width, quarter * HEAD_DIM), BF16),
             pltpu.VMEM((prompts, positions, 2, cache_width), BF16),
             pltpu.VMEM((prompts, positions, cache_width), BF16),
@@ -686,7 +685,7 @@
             pltpu.VMEM((rows, heads_per * n_col // n_row * HEAD_DIM), BF16),
             dma((2 * n_row + 2,)),
             dma,
-            dma((5,)),
+            dma((4,)),
             dma((n_col, 2)),
             dma((n_col, 2)),
             dma((2,)),
@@ -702,11 +701,11 @@
             dma((n_row,)),
             dma((n_row,)),
             dma((n_row,)),
-            dma((mine,)),
-            dma((mine,)),
+            dma((mine, prompts)),
+            dma((mine, prompts)),
         ],
         compiler_params=pltpu.CompilerParams(
-            collective_id=0, has_side_effects=True, vmem_limit_bytes=60 * 1024 * 1024
+            collective_id=0, has_side_effects=True, vmem_limit_bytes=54912 * 1024
         ),
     )(
         hidden_in[0],
@@ -716,14 +715,6 @@
         kv_cache[0],
         lengths,
     )
-    outputs = (handed, new_kv)
-    handed, new_kv = pl.pallas_call(
-        copy_both,
-        out_shape=tuple(jax.ShapeDtypeStruct(x.shape, x.dtype) for x in outputs),
-        in_specs=[pl.BlockSpec(memory_space=pl.ANY)] * 2,
-        out_specs=[pl.BlockSpec(memory_space=pltpu.HBM)] * 2,
-        scratch_shapes=[dma((2,))],
-    )(*outputs)
     return handed[None], new_kv[None]
 
 

time: 54.8 us -> 49 us (0.89)
  the two profiles are of different devices: /device:TPU:2 before, /device:TPU:17 now
where the time goes in v5:
time: 49 us; the launch traced here: 48.8 us
  Pallas kernels  45.5 us (93%)
  local copies, waits for them, and re-layouts  2.66 us (5%)
  between operations  0.65 us (1%)
    pallas_call x1, Pallas kernels, shards(): pl.pallas_call(functools.partial(kernel, dims), out_shape=(jax.ShapeDtype...  45.5 us
    unnamed x6, local copies, waits for them, and re-layouts  2.66 us

profile of v5, /device:TPU:17, one launch (start us, length us, event | category | flops | bytes accessed | tf_op | source)
XLA Modules:
  0.0 48.8 jit_solution(13676957757111496052)
XLA Ops:
  0.6 0.0 copy-start
  0.6 0.7 %copy-done = f32[1,2048]{1,0:T(1,128)S(1)} copy-done((f32[1,2048]{1,0:T(1,128)S(1)}, f32[1,2048]{1,0:T(1,128)}, u32[]{:S(2)}) %copy-start) | copy-done | bytes 8216
  1.3 0.0 copy-start.1
  1.3 0.7 %copy-done.1 = s32[1,2]{1,0:T(1,128)S(1)} copy-done((s32[1,2]{1,0:T(1,128)S(1)}, s32[1,2]{1,0:T(1,128)}, u32[]{:S(2)}) %copy-start.1) | copy-done | bytes 32
  2.0 45.5 %shard_map.77 = (bf16[32,2048]{1,0:T(8,128)(2,1)S(1)}, bf16[32,2048]{1,0:T(8,128)(2,1)S(1)}) custom-call(bf16[32,2048]{1,0:T(8,128)(2,1)} %bitcast.11, f32[1,2048]{1,0:T(1,128)S(1)} %copy-done, bf16[2048,2048]{1,0:T(8,128)(2,1)} %bitcast.8, bf16[2048,512]{1,0:T(8,128)(2,1)} %bitcast.9, bf16[2,256,2,1024]{3,2,1,0:T(2,128)(2,1)} %bitcast.10, s32[1,2]{1,0:T(1,128)S(1)} %copy-done.1), custom_call_target="tpu_custom_call" | custom-call | tf_op jit(solution)/shard_map/pallas_call | solution.py:659
  47.5 0.7 %copy.10 = bf16[1,32,2048]{2,1,0:T(8,128)(2,1)} copy(bf16[1,32,2048]{2,1,0:T(8,128)(2,1)S(1)} %bitcast.7) | data formatting | bytes 262144
  48.2 0.7 %copy.11 = bf16[1,32,2048]{2,1,0:T(8,128)(2,1)} copy(bf16[1,32,2048]{2,1,0:T(8,128)(2,1)S(1)} %bitcast.6) | data formatting | bytes 262144
Async XLA Ops:
  0.6 0.7 %copy-start = (f32[1,2048]{1,0:T(1,128)S(1)}, f32[1,2048]{1,0:T(1,128)}, u32[]{:S(2)}) copy-start(f32[1,2048]{1,0:T(1,128)} %gain_hbm.1) | copy-start | bytes 24580
  1.3 0.7 %copy-start.1 = (s32[1,2]{1,0:T(1,128)S(1)}, s32[1,2]{1,0:T(1,128)}, u32[]{:S(2)}) copy-start(s32[1,2]{1,0:T(1,128)} %len_hbm.1) | copy-start | bytes 28

commit v6 on v5

--- a/solution.py
+++ b/solution.py
@@ -108,9 +108,6 @@
                 )
             )
             taken, filled = taken + wide, filled + wide
-    for load in loads:
-        load.start()
-
     barrier = pltpu.get_barrier_semaphore()
     for d in range(1, n_row):
         pl.semaphore_signal(barrier, inc=1, device_id=(sec, peer(d), col), device_id_type=MESH)
@@ -159,6 +156,9 @@
         @pl.when(col < n_col - 1)
         def _():
             own_copy(h, above, own_send).start()
+
+    for load in loads:
+        load.start()
 
     for load in own_loads:
         load.wait()

time: 49 us -> 48.7 us (level)
  no operation moved by 1% of the time
where the time goes in v6:
time: 48.7 us; the launch traced here: 48.5 us
  Pallas kernels  45.2 us (93%)
  local copies, waits for them, and re-layouts  2.66 us (5%)
  between operations  0.65 us (1%)
    pallas_call x1, Pallas kernels, shards(): pl.pallas_call(functools.partial(kernel, dims), out_shape=(jax.ShapeDtype...  45.2 us
    unnamed x6, local copies, waits for them, and re-layouts  2.66 us

profile of v6, /device:TPU:17, one launch (start us, length us, event | category | flops | bytes accessed | tf_op | source)
XLA Modules:
  0.0 48.5 jit_solution(10831415687660198126)
XLA Ops:
  0.6 0.0 copy-start
  0.6 0.7 %copy-done = f32[1,2048]{1,0:T(1,128)S(1)} copy-done((f32[1,2048]{1,0:T(1,128)S(1)}, f32[1,2048]{1,0:T(1,128)}, u32[]{:S(2)}) %copy-start) | copy-done | bytes 8216
  1.3 0.0 copy-start.1
  1.3 0.7 %copy-done.1 = s32[1,2]{1,0:T(1,128)S(1)} copy-done((s32[1,2]{1,0:T(1,128)S(1)}, s32[1,2]{1,0:T(1,128)}, u32[]{:S(2)}) %copy-start.1) | copy-done | bytes 32
  2.0 45.2 %shard_map.77 = (bf16[32,2048]{1,0:T(8,128)(2,1)S(1)}, bf16[32,2048]{1,0:T(8,128)(2,1)S(1)}) custom-call(bf16[32,2048]{1,0:T(8,128)(2,1)} %bitcast.11, f32[1,2048]{1,0:T(1,128)S(1)} %copy-done, bf16[2048,2048]{1,0:T(8,128)(2,1)} %bitcast.8, bf16[2048,512]{1,0:T(8,128)(2,1)} %bitcast.9, bf16[2,256,2,1024]{3,2,1,0:T(2,128)(2,1)} %bitcast.10, s32[1,2]{1,0:T(1,128)S(1)} %copy-done.1), custom_call_target="tpu_custom_call" | custom-call | tf_op jit(solution)/shard_map/pallas_call | solution.py:659
  47.2 0.7 %copy.10 = bf16[1,32,2048]{2,1,0:T(8,128)(2,1)} copy(bf16[1,32,2048]{2,1,0:T(8,128)(2,1)S(1)} %bitcast.7) | data formatting | bytes 262144
  47.8 0.7 %copy.11 = bf16[1,32,2048]{2,1,0:T(8,128)(2,1)} copy(bf16[1,32,2048]{2,1,0:T(8,128)(2,1)S(1)} %bitcast.6) | data formatting | bytes 262144
Async XLA Ops:
  0.6 0.7 %copy-start = (f32[1,2048]{1,0:T(1,128)S(1)}, f32[1,2048]{1,0:T(1,128)}, u32[]{:S(2)}) copy-start(f32[1,2048]{1,0:T(1,128)} %gain_hbm.1) | copy-start | bytes 24580
  1.3 0.7 %copy-start.1 = (s32[1,2]{1,0:T(1,128)S(1)}, s32[1,2]{1,0:T(1,128)}, u32[]{:S(2)}) copy-start(s32[1,2]{1,0:T(1,128)} %len_hbm.1) | copy-start | bytes 28

commit v7 on v6

--- a/solution.py
+++ b/solution.py
@@ -272,11 +272,11 @@
 
     def spread(source):
         full_copy(source, row, across, 0).start()
+        full_copy(source, row, far_peer, 2).start()
         full_copy(source, row, mate, 1).start()
 
     def relay(source):
         full_copy(source, across, mate, 2).wait_recv()
-        full_copy(source, across, mate, 2).start()
 
     def turn_copy(block):
         return pltpu.make_async_remote_copy(
@@ -630,7 +630,7 @@
             sum_copy(block, peer(d)).wait_send()
         full_copy(block, row, across, 0).wait_send()
         full_copy(block, row, mate, 1).wait_send()
-        full_copy(block, across, mate, 2).wait_send()
+        full_copy(block, row, far_peer, 2).wait_send()
         return carry
 
     lax.fori_loop(0, n_col, drain, 0)

time: 48.7 us -> 50.3 us (1.033)
  the two profiles are of different devices: /device:TPU:17 before, /device:TPU:10 now
where the time goes in v7:
time: 50.3 us; the launch traced here: 50 us
  Pallas kernels  46.7 us (93%)
  local copies, waits for them, and re-layouts  2.66 us (5%)
  between operations  0.65 us (1%)
    pallas_call x1, Pallas kernels, shards(): pl.pallas_call(functools.partial(kernel, dims), out_shape=(jax.ShapeDtype...  46.7 us
    unnamed x6, local copies, waits for them, and re-layouts  2.66 us

profile of v7, /device:TPU:10, one launch (start us, length us, event | category | flops | bytes accessed | tf_op | source)
XLA Modules:
  0.0 50.0 jit_solution(11812648065771393747)
XLA Ops:
  0.6 0.0 copy-start
  0.6 0.7 %copy-done = f32[1,2048]{1,0:T(1,128)S(1)} copy-done((f32[1,2048]{1,0:T(1,128)S(1)}, f32[1,2048]{1,0:T(1,128)}, u32[]{:S(2)}) %copy-start) | copy-done | bytes 8216
  1.3 0.0 copy-start.1
  1.3 0.7 %copy-done.1 = s32[1,2]{1,0:T(1,128)S(1)} copy-done((s32[1,2]{1,0:T(1,128)S(1)}, s32[1,2]{1,0:T(1,128)}, u32[]{:S(2)}) %copy-start.1) | copy-done | bytes 32
  2.0 46.7 %shard_map.77 = (bf16[32,2048]{1,0:T(8,128)(2,1)S(1)}, bf16[32,2048]{1,0:T(8,128)(2,1)S(1)}) custom-call(bf16[32,2048]{1,0:T(8,128)(2,1)} %bitcast.11, f32[1,2048]{1,0:T(1,128)S(1)} %copy-done, bf16[2048,2048]{1,0:T(8,128)(2,1)} %bitcast.8, bf16[2048,512]{1,0:T(8,128)(2,1)} %bitcast.9, bf16[2,256,2,1024]{3,2,1,0:T(2,128)(2,1)} %bitcast.10, s32[1,2]{1,0:T(1,128)S(1)} %copy-done.1), custom_call_target="tpu_custom_call" | custom-call | tf_op jit(solution)/shard_map/pallas_call | solution.py:659
  48.7 0.7 %copy.10 = bf16[1,32,2048]{2,1,0:T(8,128)(2,1)} copy(bf16[1,32,2048]{2,1,0:T(8,128)(2,1)S(1)} %bitcast.7) | data formatting | bytes 262144
  49.4 0.7 %copy.11 = bf16[1,32,2048]{2,1,0:T(8,128)(2,1)} copy(bf16[1,32,2048]{2,1,0:T(8,128)(2,1)S(1)} %bitcast.6) | data formatting | bytes 262144
Async XLA Ops:
  0.6 0.7 %copy-start = (f32[1,2048]{1,0:T(1,128)S(1)}, f32[1,2048]{1,0:T(1,128)}, u32[]{:S(2)}) copy-start(f32[1,2048]{1,0:T(1,128)} %gain_hbm.1) | copy-start | bytes 24580
  1.3 0.7 %copy-start.1 = (s32[1,2]{1,0:T(1,128)S(1)}, s32[1,2]{1,0:T(1,128)}, u32[]{:S(2)}) copy-start(s32[1,2]{1,0:T(1,128)} %len_hbm.1) | copy-start | bytes 28
